TPU v7x, 128 devices: a whole 4x4x4 slice. The times are simulated.
128 devices in a mesh: qrow: 32 (over x, y_lo, z), kcol: 4 (over y_hi, core).
Axes of the slice: x: 4, y: 4 (y_hi: 2, y_lo: 2; y = y_hi * 2 + y_lo), z: 4, core: 2. Of those that a mesh axis runs over, the one named last changes fastest.
Arguments:
- queries: bfloat16 [16384, 1024], P(('qrow', 'kcol')), may hold values from -6 to 6
- key_states: bfloat16 [16384, 128], P(('qrow', 'kcol')), may hold values from -6 to 6
- value_states: bfloat16 [16384, 128], P(('qrow', 'kcol')), may hold values from -6 to 6
- out_grad: bfloat16 [16384, 1024], P(('qrow', 'kcol')), may hold values from -6 to 6
- forward_out: bfloat16 [16384, 1024], P(('qrow', 'kcol')), may hold values from -1.1953125 to 1.1953125
- stretch_order: int32 [128], replicated, may hold values from 0 to 127, each once
Outputs:
- d_query: bfloat16 [16384, 1024], P(('qrow', 'kcol'))
- d_key: bfloat16 [16384, 128], P(('qrow', 'kcol'))
- d_value: bfloat16 [16384, 128], P(('qrow', 'kcol'))
Inputs may be any that keep to these rules, and one draw needn't show every extreme that they name: `stretch_order`: every stretch number appears once.
All inputs are finite; a program needn't handle non-finite values.
Results may differ from a plain program's by a relative error of at most 0.018.
Values may be sent and summed in bfloat16 or wider, within the bound.
No kernel may reach another device: no remote copies, remote signals or barrier semaphores. Data moves between devices by JAX's collectives and lax.ppermute only.
A program may use at most 128 MiB of HBM per device.

v0:
```python
import jax
import jax.numpy as jnp
from jax import lax
from jax.sharding import PartitionSpec as P

NEGATIVE = -1e30


def joined(value, axis, combine):
    everything = jax.tree.map(lambda part: lax.all_gather(part, axis), value)
    leading = jax.tree.map(lambda part: part[0], everything)

    def step(k, so_far):
        return combine(so_far, jax.tree.map(lambda part: part[k], everything))

    return lax.fori_loop(1, lax.axis_size(axis), step, leading)


def contract(left, right, left_dim, right_dim):
    return lax.dot_general(
        left, right, (((left_dim,), (right_dim,)), ((), ())), preferred_element_type=jnp.float32
    )


def combine(first, second):
    peak = jnp.maximum(first[0], second[0])
    summed = first[1] * jnp.exp(first[0] - peak) + second[1] * jnp.exp(second[0] - peak)
    return (peak, summed)


def places_of(shard_ids, stretch_order, stretch):
    table = jnp.arange(stretch_order.shape[0], dtype=jnp.int32)
    chosen = jnp.sum(
        jnp.where(shard_ids[:, None] == table[None, :], stretch_order[None, :], 0), axis=1
    )
    return (chosen[:, None] * stretch + jnp.arange(stretch, dtype=jnp.int32)[None, :]).reshape(-1)


def softmax_totals(query_all, query_place, key_all, key_place, heads, stretch):
    width = key_all.shape[1]
    rows = query_all.shape[0]
    columns = key_all.shape[0]
    height = stretch * heads
    scale = float(width) ** (-0.5)
    query_blocks = query_all.reshape(rows // stretch, height, width)
    query_spots = jnp.repeat(query_place, heads).reshape(rows // stretch, height)
    key_blocks = key_all.reshape(columns // stretch, stretch, width)
    key_spots = key_place.reshape(columns // stretch, stretch)

    def softmax_per_query(carry, pieces):
        query_rows, query_places = pieces

        def softmax_per_key(state, key_pieces):
            key_rows, key_places = key_pieces
            scores = contract(query_rows, key_rows, 1, 1) * scale
            allowed = key_places[None, :] <= query_places[:, None]
            peak = jnp.max(jnp.where(allowed, scores, NEGATIVE), axis=1)
            summed = jnp.sum(jnp.where(allowed, jnp.exp(scores - peak[:, None]), 0.0), axis=1)
            block_stats = (peak, summed)
            return (combine(state, block_stats), None)

        start = (jnp.full((height,), NEGATIVE, jnp.float32), jnp.zeros((height,), jnp.float32))
        state, _ = lax.scan(softmax_per_key, start, (key_blocks, key_spots))
        return (carry, state)

    _, (peaks, sums) = lax.scan(
        softmax_per_query, jnp.zeros((), jnp.float32), (query_blocks, query_spots)
    )
    return (peaks.reshape(-1), sums.reshape(-1))


def gradients(
    query_all,
    grad_all,
    delta_all,
    query_place,
    log_totals,
    key_all,
    value_all,
    key_place,
    heads,
    stretch,
):
    width = key_all.shape[1]
    rows = query_all.shape[0]
    columns = key_all.shape[0]
    height = stretch * heads
    query_count = rows // stretch
    key_count = columns // stretch
    scale = float(width) ** (-0.5)
    query_blocks = query_all.reshape(query_count, height, width)
    grad_blocks = grad_all.reshape(query_count, height, width)
    delta_blocks = delta_all.reshape(query_count, height)
    log_blocks = log_totals.reshape(query_count, height)
    query_spots = jnp.repeat(query_place, heads).reshape(query_count, height)
    key_blocks = key_all.reshape(key_count, stretch, width)
    value_blocks = value_all.reshape(key_count, stretch, width)
    key_spots = key_place.reshape(key_count, stretch)

    def gradients_per_query(totals, pieces):
        query_rows, grad_rows, delta_rows, log_rows, query_places = pieces

        def gradients_per_key(query_sum, key_pieces):
            key_rows, value_rows, key_places = key_pieces
            scores = contract(query_rows, key_rows, 1, 1) * scale
            allowed = key_places[None, :] <= query_places[:, None]
            probs = jnp.where(allowed, jnp.exp(scores - log_rows[:, None]), 0.0)
            probs_low = probs.astype(jnp.bfloat16)
            value_part = contract(probs_low, grad_rows, 0, 0)
            dprobs = contract(grad_rows, value_rows, 1, 1)
            dscores = (probs * (dprobs - delta_rows.astype(jnp.float32)[:, None])).astype(
                jnp.bfloat16
            )
            query_part = jnp.dot(dscores, key_rows, preferred_element_type=jnp.float32)
            key_part = contract(dscores, query_rows, 0, 0)
            query_part, key_part, value_part = (query_part, key_part, value_part)
            return (query_sum + query_part, (key_part, value_part))

        query_sum, (key_parts, value_parts) = lax.scan(
            gradients_per_key,
            jnp.zeros((height, width), jnp.float32),
            (key_blocks, value_blocks, key_spots),
        )
        return (
            (
                totals[0] + key_parts.reshape(columns, width),
                totals[1] + value_parts.reshape(columns, width),
            ),
            query_sum,
        )

    zeros = jnp.zeros((columns, width), jnp.float32)
    (key_total, value_total), query_sums = lax.scan(
        gradients_per_query,
        (zeros, zeros),
        (query_blocks, grad_blocks, delta_blocks, log_blocks, query_spots),
    )
    return (query_sums.reshape(rows, heads * width) * scale, key_total * scale, value_total)


def shards(queries, key_states, value_states, out_grad, forward_out, stretch_order):
    stretch = queries.shape[0]
    width = key_states.shape[1]
    heads = queries.shape[1] // width
    row_count = lax.axis_size("qrow")
    column_count = lax.axis_size("kcol")
    row_index = lax.axis_index("qrow")
    column_index = lax.axis_index("kcol")
    products = out_grad.astype(jnp.float32) * forward_out.astype(jnp.float32)
    delta = jnp.sum(products.reshape(stretch, heads, width), axis=2).astype(jnp.bfloat16)
    along_rows = jnp.arange(row_count, dtype=jnp.int32) * column_count + column_index
    along_columns = row_index * column_count + jnp.arange(column_count, dtype=jnp.int32)
    query_all, grad_all, delta_all = (
        lax.all_gather(queries, "qrow", axis=0, tiled=True),
        lax.all_gather(out_grad, "qrow", axis=0, tiled=True),
        lax.all_gather(delta, "qrow", axis=0, tiled=True),
    )
    key_all, value_all = (
        lax.all_gather(key_states, "kcol", axis=0, tiled=True),
        lax.all_gather(value_states, "kcol", axis=0, tiled=True),
    )
    query_place = places_of(along_rows, stretch_order, stretch)
    key_place = places_of(along_columns, stretch_order, stretch)
    peaks, sums = softmax_totals(query_all, query_place, key_all, key_place, heads, stretch)
    peaks, sums = joined((peaks, sums), "qrow", combine)
    log_totals = peaks + jnp.log(sums)
    query_grad, key_grad, value_grad = gradients(
        query_all,
        grad_all,
        delta_all,
        query_place,
        log_totals,
        key_all,
        value_all,
        key_place,
        heads,
        stretch,
    )
    d_query = lax.psum_scatter(
        query_grad.astype(jnp.bfloat16), "qrow", scatter_dimension=0, tiled=True
    )
    d_key, d_value = (
        lax.psum_scatter(
            key_grad.astype(jnp.bfloat16), "kcol", scatter_dimension=0, tiled=True
        ).astype(jnp.float32),
        lax.psum_scatter(
            value_grad.astype(jnp.bfloat16), "kcol", scatter_dimension=0, tiled=True
        ).astype(jnp.float32),
    )
    return (d_query, d_key.astype(jnp.bfloat16), d_value.astype(jnp.bfloat16))


def solution(mesh):
    in_specs = (
        P(("qrow", "kcol"), None),
        P(("qrow", "kcol"), None),
        P(("qrow", "kcol"), None),
        P(("qrow", "kcol"), None),
        P(("qrow", "kcol"), None),
        P(),
    )
    out_specs = (P(("qrow", "kcol"), None), P(("qrow", "kcol"), None), P(("qrow", "kcol"), None))
    return jax.shard_map(shards, mesh=mesh, in_specs=in_specs, out_specs=out_specs, check_vma=False)
```

profile of v0, /device:TPU:0, one launch (start us, length us, event | category | flops | bytes accessed | tf_op | source)
XLA Modules:
  0.0 1249.9 jit_solution(15080808206441747653)
XLA Ops:
  10.4 7.1 all_gather.22
  17.8 161.5 %all-gather.7.cloned.1.call-done = bf16[4096,1024]{1,0:T(8,128)(2,1)} async-done(((bf16[128,1024]{1,0:T(8,128)(2,1)}), bf16[4096,1024]{1,0:T(8,128)(2,1)}) %all-gather.7.cloned.1.call-update) | async-done | bytes 8388624 | tf_op jit(solution)/shard_map/all_gather | solution.py:154
  179.3 13.4 %reshape.69 = bf16[32,1024,128]{2,1,0:T(8,128)(2,1)} reshape(bf16[4096,1024]{1,0:T(8,128)(2,1)} %all-gather.7.cloned.1.call-done) | data formatting | bytes 16777216 | tf_op jit(solution)/shard_map/reshape | solution.py:91
  192.6 100.6 %while.77 = (s32[]{:T(128)}, f32[32,1024]{1,0:T(8,128)S(1)}, f32[32,1024]{1,0:T(8,128)S(1)}, bf16[32,1024,128]{2,1,0:T(8,128)(2,1)}, s32[32,1024]{1,0:T(8,128)S(...) while((s32[]{:T(128)}, f32[32,1024]{1,0:T(8,128)S(1)}, ...), condition=%wide.region_8.9_spmd.clone, body=%wide.region_3.8_spmd.clone.sunk | while | flops 34609664 | bytes 1941852 | solution.py:66
  295.4 89.2 %all_gather.26 = bf16[4096,8]{1,0:T(8,128)(2,1)S(1)} all-gather(bf16[128,8]{1,0:T(8,128)(2,1)S(1)} %reduce_sum.38), channel_id=1, replica_groups=mesh['qrow'=32,'kcol'=4] {'qrow'}, dimensions={0}, use_global_device_ids=true | all-gather | bytes 67584 | tf_op jit(solution)/shard_map/all_gather | solution.py:156
  386.1 8.8 all_gather.27
  394.9 13.3 %reshape.72 = bf16[32,1024,128]{2,1,0:T(8,128)(2,1)} reshape(bf16[4096,1024]{1,0:T(8,128)(2,1)} %all-gather.9.cloned.1.call-done) | data formatting | bytes 16777216 | tf_op jit(solution)/shard_map/reshape | solution.py:92
  408.2 101.1 %all-gather.13.cloned.1.call-done = f32[32,1,32768]{2,1,0:T(1,128)} async-done(((f32[1,1,32768]{2,1,0:T(1,128)}), f32[32,1,32768]{2,1,0:T(1,128)}) %all-gather.13.cloned.1.call-update) | async-done | bytes 4194320 | tf_op jit(solution)/shard_map/all_gather | solution.py:10
  509.4 6.6 copy.24
  516.0 153.2 %all-gather.11.cloned.1.call-done = f32[32,1,32768]{2,1,0:T(1,128)} async-done(((f32[1,1,32768]{2,1,0:T(1,128)}), f32[32,1,32768]{2,1,0:T(1,128)}) %all-gather.11.cloned.1.call-update) | async-done | bytes 4194320 | tf_op jit(solution)/shard_map/all_gather | solution.py:10
  669.2 6.7 copy.25
  675.9 57.9 %while.75 = (s32[]{:T(128)}, f32[32768]{0:T(1024)S(1)}, f32[32768]{0:T(1024)S(1)}, f32[32,32768]{1,0:T(8,128)}, f32[32,32768]{1,0:T(8,128)}, /*index=5*/s32[]{:T(128)}, s32[]{:T(128)}, s32[]{:T(128)}) while((s32[]{:T(128)}, f32[32768]{0:T(1024)S(1)}, f32[32768]{0:T(1024)S(1)}, f32[32,32768]{1,0:T(8,128)}, f32[32,32768]{1,0:T(8,128)}, ...), condition=%wide.region_10.11_spmd, body=%wide.region_9.10_spmd.sunk | while | flops 196613 | bytes 1310843 | solution.py:16
  733.9 271.1 %while.79 = (s32[]{:T(128)}, f32[512,128]{1,0:T(8,128)S(1)}, f32[512,128]{1,0:T(8,128)S(1)}, f32[32,1024,128]{2,1,0:T(8,128)}, bf16[32,1024,128]{2,1,0:T(8,128)(...) while((s32[]{:T(128)}, f32[512,128]{1,0:T(8,128)S(1)}, ...), condition=%wide.region_14.15_spmd.clone, body=%wide.region_11.14_spmd.clone.sunk | while | flops 169346560 | bytes 8398838 | solution.py:133
  736.0 5.4 while.81
  744.5 5.4 while.81
  752.9 5.4 while.81
  761.4 5.4 while.81
  769.9 5.4 while.81
  778.3 5.4 while.81
  786.8 5.4 while.81
  795.3 5.4 while.81
  803.8 5.4 while.81
  812.2 5.4 while.81
  820.7 5.4 while.81
  829.2 5.4 while.81
  837.6 5.4 while.81
  846.1 5.4 while.81
  854.6 5.4 while.81
  863.0 5.4 while.81
  871.6 5.4 while.81
  880.1 5.4 while.81
  888.5 5.4 while.81
  905.5 5.4 while.81
  914.0 5.4 while.81
  922.4 5.4 while.81
  930.9 5.4 while.81
  939.3 5.4 while.81
  947.8 5.4 while.81
  956.3 5.4 while.81
  964.8 5.4 while.81
  973.2 5.4 while.81
  981.7 5.4 while.81
  990.2 5.4 while.81
  998.7 5.4 while.81
  1006.5 9.4 multiply_convert_fusion
  1015.9 13.4 %convert_element_type.42 = bf16[4096,1024]{1,0:T(8,128)(2,1)} reshape(bf16[32,1024,128]{2,1,0:T(8,128)(2,1)} %multiply_convert_fusion) | data formatting | bytes 16777216 | tf_op jit(solution)/shard_map/convert_element_type | solution.py:180
  1031.9 29.1 %reduce-scatter.8.cloned.1.call-done = bf16[128,128]{1,0:T(8,128)(2,1)} async-done(((bf16[512,128]{1,0:T(8,128)(2,1)}), bf16[128,128]{1,0:T(8,128)(2,1)}) %reduce-scatter.8.cloned.1.call-update) | async-done | bytes 32784 | tf_op jit(solution)/shard_map/reduce_scatter | solution.py:186
  1061.0 182.1 %reduce-scatter.4.cloned.1.call-done = bf16[128,1024]{1,0:T(8,128)(2,1)} async-done(((bf16[4096,1024]{1,0:T(8,128)(2,1)}), bf16[128,1024]{1,0:T(8,128)(2,1)}) %reduce-scatter.4.cloned.1.call-update) | async-done | bytes 262160 | tf_op jit(solution)/shard_map/reduce_scatter | solution.py:179
  (2129 shorter events, 485.5 us)
Async XLA Ops:
  7.2 172.1 %all-gather.7.cloned.1.call-start = ((), (), s32[]{:S(2)}) async-start(), calls=%async_computation.3 | async-start | bytes 8650752 | tf_op jit(solution)/shard_map/all_gather | solution.py:154
  7.9 387.0 %all-gather.9.cloned.1.call-start = ((), (), s32[]{:S(2)}) async-start(), calls=%async_computation.4 | async-start | bytes 8650752 | tf_op jit(solution)/shard_map/all_gather | solution.py:155
  8.6 500.7 %all-gather.13.cloned.1.call-start = ((), (), s32[]{:S(2)}) async-start(), calls=%async_computation.9 | async-start | bytes 4325376 | tf_op jit(solution)/shard_map/all_gather | solution.py:10
  192.6 102.4 %copy-start = (bf16[128,1024]{1,0:T(8,128)(2,1)S(1)}, bf16[128,1024]{1,0:T(8,128)(2,1)}, u32[]{:S(2)}) copy-start(bf16[128,1024]{1,0:T(8,128)(2,1)} %param.19) | copy-start | bytes 786436
  192.6 102.4 %copy-start.1 = (bf16[128,1024]{1,0:T(8,128)(2,1)S(1)}, bf16[128,1024]{1,0:T(8,128)(2,1)}, u32[]{:S(2)}) copy-start(bf16[128,1024]{1,0:T(8,128)(2,1)} %param.20) | copy-start | bytes 786436
  192.6 193.5 %copy-start.2 = (bf16[128,128]{1,0:T(8,128)(2,1)S(1)}, bf16[128,128]{1,0:T(8,128)(2,1)}, u32[]{:S(2)}) copy-start(bf16[128,128]{1,0:T(8,128)(2,1)} %param.18) | copy-start | bytes 98308
  294.0 375.1 %all-gather.11.cloned.1.call-start = ((), (), s32[]{:S(2)}) async-start(), calls=%async_computation.8 | async-start | bytes 4325376 | tf_op jit(solution)/shard_map/all_gather | solution.py:10
  294.9 737.0 %reduce-scatter.6.cloned.1.call-start = ((), (), s32[]{:S(2)}) async-start(), calls=%async_computation.6 | async-start | bytes 163840 | tf_op jit(solution)/shard_map/reduce_scatter | solution.py:183
  509.4 166.5 %slice-start = ((f32[32,1,32768]{2,1,0:T(1,128)}), f32[1,1,32768]{2,1,0:T(1,128)S(1)}, s32[]{:S(2)}) async-start(f32[32,1,32768]{2,1,0:T(1,128)} %all-gather.13.cloned.1.call-done), calls=%async_computation.10 | async-start | bytes 262144 | tf_op jit(solution)/shard_map/slice | solution.py:11
  669.2 6.8 slice-start.1
  1005.7 55.3 %reduce-scatter.8.cloned.1.call-start = ((), (), s32[]{:S(2)}) async-start(), calls=%async_computation.7 | async-start | bytes 163840 | tf_op jit(solution)/shard_map/reduce_scatter | solution.py:186
  1006.4 236.6 %reduce-scatter.4.cloned.1.call-start = ((), (), s32[]{:S(2)}) async-start(), calls=%async_computation.5 | async-start | bytes 8650752 | tf_op jit(solution)/shard_map/reduce_scatter | solution.py:179
Sparse Core Ops, SparseCore 0:
  9.6 169.5 all-gather.6
  180.9 171.0 all-gather.8
  353.6 155.7 all-gather.12
  511.4 157.6 all-gather.10
  1005.8 26.0 reduce-scatter.5
  1035.0 25.9 reduce-scatter.7
  1063.9 179.0 reduce-scatter.3
where the time goes:
time: 1250 us
  waiting for transfers between devices  631 us (50%)
  local copies, waits for them, and re-layouts  242 us (19%)
  matrix products  194 us (16%)
  blocking collectives  105 us (8%)
  other arithmetic  45.1 us (4%)
  loops' own time  18.6 us (1%)
  between operations  14.3 us (1%)
    all_gather x2, waiting for transfers between devices, joined(): everything = jax.tree.map(lambda part: lax.all_gather(part, axis), value)  254 us
    reduce_scatter x1, waiting for transfers between devices, shards(): lax.psum_scatter(query_grad.astype(jnp.bfloat16), 'qrow', scatter_dimensi...  182 us
    all_gather x1, waiting for transfers between devices, shards(): lax.all_gather(queries, 'qrow', axis=0, tiled=True)  161 us
    dot_general x640, matrix products, contract(): lax.dot_general(left, right, (((left_dim,), (right_dim,)), ((), ())), pre...  154 us
    squeeze x96, local copies, waits for them, and re-layouts, softmax_totals(): lax.scan(softmax_per_query, jnp.zeros((), jnp.float32), (query_blocks, qu...  93.6 us
    all_gather x1, blocking collectives, shards(): lax.all_gather(delta, 'qrow', axis=0, tiled=True)  89.2 us
    dynamic_slice x31, local copies, waits for them, and re-layouts, step(): return combine(so_far, jax.tree.map(lambda part: part[k], everything))  53.6 us
    dot_general x128, matrix products, gradients_per_key(): query_part = jnp.dot(dscores, key_rows, preferred_element_type=jnp.float32)  39.6 us
  transfers between devices with their start and end apart: 7, of which 6 were waited for; matrix products, arithmetic and copies ran while one was open for 12% of the time, Pallas kernels for 0%

commit v1 on v0

v1 whole, which is shorter than its diff:
```python
import jax
import jax.numpy as jnp
from jax import lax
from jax.experimental import pallas as pl
from jax.experimental.pallas import tpu as pltpu
from jax.sharding import PartitionSpec as P

ALL = ("qrow", "kcol")
DEVICES = 128
HEADS = 8
WIDTH = 128
STRETCH = 128
PLACES = 128
KEY_GROUPS = 4
ROW_GROUPS = 32
QUERY_TOKENS = STRETCH // ROW_GROUPS
KEY_TOKENS = STRETCH // KEY_GROUPS
HALF = KEY_TOKENS // 2
ROWS = QUERY_TOKENS * HEADS
ALL_ROWS = PLACES * ROWS
ALL_KEYS = PLACES * KEY_TOKENS
TILE = 512
TILES = ALL_ROWS // TILE
SPAN = TILE // ROWS
NEGATIVE = -1e30
SCALE = float(WIDTH) ** (-0.5)
TO_LOG2 = SCALE * 1.4426950408889634
VMEM = 56 * 1024 * 1024


def contract(left, right, left_dim, right_dim):
    return lax.dot_general(
        left, right, (((left_dim,), (right_dim,)), ((), ())), preferred_element_type=jnp.float32
    )


def tile_at(index):
    return pl.ds(pl.multiple_of(index * TILE, TILE), TILE)


def allowed_on_diagonal(key_group, row_group):
    row = lax.broadcasted_iota(jnp.int32, (TILE, TILE), 0)
    column = lax.broadcasted_iota(jnp.int32, (TILE, TILE), 1)
    row_place = (row // ROWS) * STRETCH + row_group * QUERY_TOKENS + (row % ROWS) // HEADS
    key_place = (column // KEY_TOKENS) * STRETCH + key_group * KEY_TOKENS + column % KEY_TOKENS
    return key_place <= row_place


def stats_kernel(table, moved, other_half, stats, query, key, peak, total):
    key_group, row_group, core = table[PLACES], table[PLACES + 1], table[PLACES + 2]

    def sort(place, carry):
        source = table[place]
        query[pl.ds(pl.multiple_of(place * ROWS, ROWS), ROWS)] = moved[source, 0:ROWS]
        first = pl.multiple_of(place * KEY_TOKENS + core * HALF, HALF)
        second = pl.multiple_of(place * KEY_TOKENS + (1 - core) * HALF, HALF)
        key[pl.ds(first, HALF)] = moved[source, 2 * ROWS : 2 * ROWS + HALF]
        key[pl.ds(second, HALF)] = other_half[source, 0:HALF]
        return carry

    lax.fori_loop(0, PLACES, sort, 0)
    lane = lax.broadcasted_iota(jnp.int32, (TILE, WIDTH), 1)

    def per_row_tile(i, packed):
        rows = query[tile_at(i)]
        peak[...] = jnp.full_like(peak, NEGATIVE)
        total[...] = jnp.zeros_like(total)

        def absorb(scores):
            parts = [scores[:, k * WIDTH : (k + 1) * WIDTH] for k in range(TILE // WIDTH)]
            highest = peak[...]
            old = highest
            for part in parts:
                highest = jnp.maximum(highest, part)
            summed = total[...] * jnp.exp2((old - highest) * TO_LOG2)
            for part in parts:
                summed = summed + jnp.exp2((part - highest) * TO_LOG2)
            peak[...] = highest
            total[...] = summed

        def full_tile(j, carry):
            absorb(contract(rows, key[tile_at(j)], 1, 1))
            return carry

        lax.fori_loop(0, i, full_tile, 0)
        scores = contract(rows, key[tile_at(i)], 1, 1)
        absorb(jnp.where(allowed_on_diagonal(key_group, row_group), scores, NEGATIVE))
        row_peak = jnp.max(peak[...], axis=1, keepdims=True)
        row_total = jnp.sum(
            total[...] * jnp.exp2((peak[...] - row_peak) * TO_LOG2), axis=1, keepdims=True
        )
        packed = jnp.where(lane == i, row_peak, packed)
        return jnp.where(lane == i + TILES, row_total, packed)

    packed = lax.fori_loop(0, TILES, per_row_tile, jnp.zeros((TILE, WIDTH), jnp.float32))
    stats[...] = packed.T[0 : 2 * TILES]


def gradient_kernel(
    table,
    moved,
    other_half,
    delta,
    stats_0,
    stats_1,
    stats_2,
    stats_3,
    query_grad,
    own_grad,
    other_grad,
    query,
    grad,
    key,
    value,
    query_turned,
    grad_turned,
    logs,
    query_total,
    key_total,
    value_total,
    key_sorted,
    value_sorted,
):
    key_group, row_group, core = table[PLACES], table[PLACES + 1], table[PLACES + 2]
    lane = lax.broadcasted_iota(jnp.int32, (TILE, WIDTH), 1)
    all_stats = [ref[...] for ref in (stats_0, stats_1, stats_2, stats_3)]
    peaks = [part[0:TILES] for part in all_stats]
    highest = jnp.maximum(jnp.maximum(peaks[0], peaks[1]), jnp.maximum(peaks[2], peaks[3]))
    summed = jnp.zeros_like(highest)
    for part in all_stats:
        summed = summed + part[TILES:] * jnp.exp2((part[0:TILES] - highest) * TO_LOG2)
    log_totals = highest + jnp.log2(summed) * (1.0 / TO_LOG2)
    high = log_totals.astype(jnp.bfloat16).astype(jnp.float32)
    middle = (log_totals - high).astype(jnp.bfloat16).astype(jnp.float32)
    low = (log_totals - high - middle).astype(jnp.bfloat16).astype(jnp.float32)
    padding = jnp.zeros((WIDTH - 3 * TILES, TILE), jnp.float32)
    logs[...] = jnp.concatenate([high, middle, low, padding], axis=0).T

    extra_lane = lax.broadcasted_iota(jnp.int32, (ALL_KEYS, WIDTH), 1)
    key[:, WIDTH:] = jnp.where(extra_lane < 3 * TILES, -1.0, 0.0).astype(jnp.bfloat16)
    value[:, WIDTH:] = jnp.where(extra_lane < ROWS, -1.0, 0.0).astype(jnp.bfloat16)
    row_sub = lax.broadcasted_iota(jnp.int32, (ROWS, WIDTH), 0)
    row_lane = lax.broadcasted_iota(jnp.int32, (ROWS, WIDTH), 1)

    def sort(place, carry):
        source = table[place]
        spot = pl.ds(pl.multiple_of(place * ROWS, ROWS), ROWS)
        query[spot, 0:WIDTH] = moved[source, 0:ROWS]
        grad[spot, 0:WIDTH] = moved[source, ROWS : 2 * ROWS]
        grad[spot, WIDTH:] = jnp.where(
            row_sub == row_lane, jnp.broadcast_to(delta[pl.ds(source, 1)], (ROWS, WIDTH)), 0.0
        ).astype(jnp.bfloat16)
        first = pl.ds(pl.multiple_of(place * KEY_TOKENS + core * HALF, HALF), HALF)
        second = pl.ds(pl.multiple_of(place * KEY_TOKENS + (1 - core) * HALF, HALF), HALF)
        key[first, 0:WIDTH] = moved[source, 2 * ROWS : 2 * ROWS + HALF]
        key[second, 0:WIDTH] = other_half[source, 0:HALF]
        value[first, 0:WIDTH] = moved[source, 2 * ROWS + HALF : 2 * ROWS + 2 * HALF]
        value[second, 0:WIDTH] = other_half[source, HALF : 2 * HALF]
        return carry

    lax.fori_loop(0, PLACES, sort, 0)
    key_total[...] = jnp.zeros_like(key_total)
    value_total[...] = jnp.zeros_like(value_total)

    def per_row_tile(i, carry):
        here = tile_at(i)
        chosen = jnp.logical_and(lane % TILES == i, lane < 3 * TILES)
        query[here, WIDTH:] = jnp.where(chosen, logs[...], 0.0).astype(jnp.bfloat16)
        query_turned[...] = query[here, 0:WIDTH].T
        grad_turned[...] = grad[here, 0:WIDTH].T
        query_total[...] = jnp.zeros_like(query_total)

        def tile(j, allowed):
            there = tile_at(j)
            probs = jnp.exp2(contract(query[here], key[there], 1, 1) * TO_LOG2)
            if allowed is not None:
                probs = jnp.where(allowed, probs, 0.0)
            moved_probs = contract(grad[here], value[there], 1, 1)
            dscores = (probs * moved_probs).astype(jnp.bfloat16)
            probs_low = probs.astype(jnp.bfloat16)
            value_total[:, there] += contract(grad_turned[...], probs_low, 1, 0)
            key_total[:, there] += contract(query_turned[...], dscores, 1, 0)
            query_total[...] += contract(dscores, key[there, 0:WIDTH], 1, 0)

        def full_tile(j, inner):
            tile(j, None)
            return inner

        lax.fori_loop(0, i, full_tile, 0)
        tile(i, allowed_on_diagonal(key_group, row_group))

        for k in range(SPAN):
            source = table[i * SPAN + k]
            query_grad[source] = (query_total[k * ROWS : (k + 1) * ROWS] * SCALE).astype(
                jnp.bfloat16
            )
        return carry

    lax.fori_loop(0, TILES, per_row_tile, 0)

    def turn(j, carry):
        there = tile_at(j)
        key_sorted[there] = key_total[:, there].T * SCALE
        value_sorted[there] = value_total[:, there].T
        return carry

    lax.fori_loop(0, TILES, turn, 0)

    def unsort(place, carry):
        source = table[place]
        first = pl.ds(pl.multiple_of(place * KEY_TOKENS + core * HALF, HALF), HALF)
        second = pl.ds(pl.multiple_of(place * KEY_TOKENS + (1 - core) * HALF, HALF), HALF)
        own_grad[source, 0:HALF] = key_sorted[first].astype(jnp.bfloat16)
        own_grad[source, HALF:] = value_sorted[first].astype(jnp.bfloat16)
        other_grad[source, 0:HALF] = key_sorted[second].astype(jnp.bfloat16)
        other_grad[source, HALF:] = value_sorted[second].astype(jnp.bfloat16)
        return carry

    lax.fori_loop(0, PLACES, unsort, 0)


IN_VMEM = pl.BlockSpec(memory_space=pltpu.VMEM)
IN_SMEM = pl.BlockSpec(memory_space=pltpu.SMEM)
PAIRS = TILE * TILE * TILES * (TILES + 1) // 2


def stats_call(table, moved, other_half):
    return pl.pallas_call(
        stats_kernel,
        out_shape=jax.ShapeDtypeStruct((2 * TILES, TILE), jnp.float32),
        in_specs=[IN_SMEM, IN_VMEM, IN_VMEM],
        out_specs=IN_VMEM,
        scratch_shapes=[
            pltpu.VMEM((ALL_ROWS, WIDTH), jnp.bfloat16),
            pltpu.VMEM((ALL_KEYS, WIDTH), jnp.bfloat16),
            pltpu.VMEM((TILE, WIDTH), jnp.float32),
            pltpu.VMEM((TILE, WIDTH), jnp.float32),
        ],
        compiler_params=pltpu.CompilerParams(vmem_limit_bytes=VMEM),
        cost_estimate=pl.CostEstimate(
            flops=2 * PAIRS * WIDTH, bytes_accessed=4 << 20, transcendentals=PAIRS
        ),
        name="softmax_totals",
    )(table, moved, other_half)


def gradient_call(table, moved, other_half, delta, stats):
    chunk = jax.ShapeDtypeStruct((PLACES, ROWS, WIDTH), jnp.bfloat16)
    return pl.pallas_call(
        gradient_kernel,
        out_shape=(chunk, chunk, chunk),
        in_specs=[IN_SMEM] + [IN_VMEM] * 7,
        out_specs=(IN_VMEM,) * 3,
        scratch_shapes=[
            pltpu.VMEM((ALL_ROWS, 2 * WIDTH), jnp.bfloat16),
            pltpu.VMEM((ALL_ROWS, 2 * WIDTH), jnp.bfloat16),
            pltpu.VMEM((ALL_KEYS, 2 * WIDTH), jnp.bfloat16),
            pltpu.VMEM((ALL_KEYS, 2 * WIDTH), jnp.bfloat16),
            pltpu.VMEM((WIDTH, TILE), jnp.bfloat16),
            pltpu.VMEM((WIDTH, TILE), jnp.bfloat16),
            pltpu.VMEM((TILE, WIDTH), jnp.float32),
            pltpu.VMEM((TILE, WIDTH), jnp.float32),
            pltpu.VMEM((WIDTH, ALL_KEYS), jnp.float32),
            pltpu.VMEM((WIDTH, ALL_KEYS), jnp.float32),
            pltpu.VMEM((ALL_KEYS, WIDTH), jnp.float32),
            pltpu.VMEM((ALL_KEYS, WIDTH), jnp.float32),
        ],
        compiler_params=pltpu.CompilerParams(vmem_limit_bytes=VMEM),
        cost_estimate=pl.CostEstimate(
            flops=10 * PAIRS * WIDTH, bytes_accessed=8 << 20, transcendentals=PAIRS
        ),
        name="gradients",
    )(table, moved, other_half, delta, *stats)


def shards(queries, key_states, value_states, out_grad, forward_out, stretch_order):
    me = lax.axis_index(ALL)
    swap = [(d, d ^ 1) for d in range(DEVICES)]

    def around(step):
        return [(d, (d + step * ROW_GROUPS) % DEVICES) for d in range(DEVICES)]

    with jax.named_scope("outgoing"):
        products = out_grad.astype(jnp.float32) * forward_out.astype(jnp.float32)
        delta = jnp.sum(products.reshape(STRETCH, HEADS, WIDTH), axis=2).astype(jnp.bfloat16)
        delta = jnp.pad(delta.reshape(ROW_GROUPS, 1, ROWS), ((0, 0), (0, 7), (0, WIDTH - ROWS)))
        by_row_group = jnp.concatenate(
            [
                queries.reshape(ROW_GROUPS, ROWS, WIDTH),
                out_grad.reshape(ROW_GROUPS, ROWS, WIDTH),
            ],
            axis=1,
        )
        by_key_part = jnp.concatenate(
            [
                key_states.reshape(KEY_GROUPS, 1, 2, HALF, WIDTH),
                value_states.reshape(KEY_GROUPS, 1, 2, HALF, WIDTH),
            ],
            axis=3,
        )
        spread = (KEY_GROUPS, ROW_GROUPS // 2, 2, 2 * HALF, WIDTH)
        outgoing = jnp.concatenate(
            [
                jnp.tile(by_row_group, (KEY_GROUPS, 1, 1)),
                jnp.broadcast_to(by_key_part, spread).reshape(DEVICES, 2 * HALF, WIDTH),
                jnp.tile(delta, (KEY_GROUPS, 1, 1)),
            ],
            axis=1,
        )
    with jax.named_scope("exchange_in"):
        moved = lax.all_to_all(outgoing, ALL, split_axis=0, concat_axis=0, tiled=True)
        other_half = lax.ppermute(moved[:, 2 * ROWS : 2 * ROWS + 2 * HALF], ALL, swap)
    with jax.named_scope("table"):
        places = jnp.arange(PLACES, dtype=jnp.int32)
        holder = jnp.sum(
            jnp.where(stretch_order[None, :] == places[:, None], places[None, :], 0), axis=1
        )
        ids = jnp.stack([me // ROW_GROUPS, me % ROW_GROUPS, me % 2]).astype(jnp.int32)
        table = jnp.concatenate([holder, ids])
        delta_in = moved[:, 2 * ROWS + 2 * HALF, :].astype(jnp.float32)
    with jax.named_scope("totals"):
        stats = stats_call(table, moved, other_half)
        all_stats = [stats] + [lax.ppermute(stats, ALL, around(k)) for k in range(1, KEY_GROUPS)]
    with jax.named_scope("gradients"):
        query_grad, own_grad, other_grad = gradient_call(
            table, moved, other_half, delta_in, all_stats
        )
    with jax.named_scope("exchange_out"):
        received = lax.ppermute(other_grad, ALL, swap)
        pair_grad = (own_grad.astype(jnp.float32) + received.astype(jnp.float32)).astype(
            jnp.bfloat16
        )
        back = lax.all_to_all(
            jnp.concatenate([query_grad, pair_grad], axis=1),
            ALL,
            split_axis=0,
            concat_axis=0,
            tiled=True,
        ).astype(jnp.float32)
    with jax.named_scope("sums"):
        d_query = jnp.sum(
            back[:, 0:ROWS].reshape(KEY_GROUPS, ROW_GROUPS, ROWS, WIDTH), axis=0
        ).reshape(STRETCH, HEADS * WIDTH)
        d_pair = jnp.sum(
            back[:, ROWS:].reshape(KEY_GROUPS, ROW_GROUPS // 2, 2, 2, HALF, WIDTH), axis=1
        )
        d_key = d_pair[:, :, 0].reshape(STRETCH, WIDTH)
        d_value = d_pair[:, :, 1].reshape(STRETCH, WIDTH)
    return tuple(part.astype(jnp.bfloat16) for part in (d_query, d_key, d_value))


def solution(mesh):
    split = P(ALL, None)
    return jax.shard_map(
        shards,
        mesh=mesh,
        in_specs=(split,) * 5 + (P(),),
        out_specs=(split,) * 3,
        check_vma=False,
    )
```

time: 1250 us -> 177 us (0.14)
  waiting for transfers between devices: 631 us -> 8.94 us
  local copies, waits for them, and re-layouts: 242 us -> 8.29 us
  matrix products: 194 us -> 0 us
  Pallas kernels: 0 us -> 59 us
  other arithmetic: 45.1 us -> 6.93 us
  loops' own time: 18.6 us -> 0 us
  blocking collectives: 105 us -> 88.6 us
  between operations: 14.3 us -> 0.79 us
    all_gather x4 -> x0, waiting for transfers between devices: 416 us -> none  [the longest x2 254 us: joined(): everything = jax.tree.map(lambda part: lax.all_gather(part, axis), value)]
    reduce_scatter x3 -> x0, waiting for transfers between devices: 214 us -> none  [the longest x1 182 us: shards(): lax.psum_scatter(query_grad.astype(jnp.bfloat16), 'qrow', scatter_dimensi...]
    dot_general x768 -> x0, matrix products: 194 us -> none  [the longest x640 154 us: contract(): lax.dot_general(left, right, (((left_dim,), (right_dim,)), ((), ())), pre...]
    all_gather x3 -> x0, blocking collectives: 105 us -> none  [the longest x1 89.2 us: shards(): lax.all_gather(delta, 'qrow', axis=0, tiled=True)]
    squeeze x96 -> x0, local copies, waits for them, and re-layouts: 93.6 us -> none  [softmax_totals(): lax.scan(softmax_per_query, jnp.zeros((), jnp.float32), (query_blocks, qu...]
    all_to_all x0 -> x2, blocking collectives: none -> 88.6 us  [the longest x1 54.5 us: shards(): lax.all_to_all(outgoing, ALL, split_axis=0, concat_axis=0, tiled=True)]
    pallas_call x0 -> x2, Pallas kernels: none -> 59 us  [the longest x1 38.3 us: gradient_call(): pl.pallas_call(gradient_kernel, out_shape=(chunk, chunk, chunk), in_specs...]
    dynamic_slice x159 -> x0, local copies, waits for them, and re-layouts: 55.5 us -> none  [the longest x31 53.6 us: step(): return combine(so_far, jax.tree.map(lambda part: part[k], everything))]
  transfers between devices with their start and end apart: 7 -> 5, of which waited for: 6 -> 4; matrix products, arithmetic and copies ran while one was open for 12% -> 1% of each run, Pallas kernels for 0% -> 0%
where the time goes in v1:
time: 177 us; the launch traced here: 176 us
  blocking collectives  88.6 us (50%)
  Pallas kernels  59 us (33%)
  waiting for transfers between devices  8.94 us (5%)
  local copies, waits for them, and re-layouts  8.29 us (5%)
  other arithmetic  6.93 us (4%)
  starting transfers between devices  3.62 us (2%)
    all_to_all x1, blocking collectives, shards(): lax.all_to_all(outgoing, ALL, split_axis=0, concat_axis=0, tiled=True)  54.5 us
    pallas_call x1, Pallas kernels, gradient_call(): pl.pallas_call(gradient_kernel, out_shape=(chunk, chunk, chunk), in_specs...  38.3 us
    all_to_all x1, blocking collectives, shards(): lax.all_to_all(jnp.concatenate([query_grad, pair_grad], axis=1), ALL, spl...  34.2 us
    pallas_call x1, Pallas kernels, stats_call(): pl.pallas_call(stats_kernel, out_shape=jax.ShapeDtypeStruct((2 * TILES, T...  20.7 us
    ppermute x3, waiting for transfers between devices, shards(): lax.ppermute(stats, ALL, around(k))  3.89 us
    ppermute x3, starting transfers between devices, shards(): lax.ppermute(stats, ALL, around(k))  3.61 us
  transfers between devices with their start and end apart: 5, of which 4 were waited for; matrix products, arithmetic and copies ran while one was open for 1% of the time, Pallas kernels for 0%

profile of v1, /device:TPU:0, one launch (start us, length us, event | category | flops | bytes accessed | tf_op | source)
XLA Modules:
  0.0 176.2 jit_solution(16660058364063957692)
XLA Ops:
  0.6 0.0 copy-start.2
  0.6 0.0 copy-start.3
  0.7 1.1 reshape.57
  1.7 1.1 reshape.58
  2.8 1.1 multiply_bitcast_fusion
  3.9 0.1 copy.27
  4.0 0.2 reduce_sum.37
  4.2 0.1 convert_element_type.67
  4.3 0.0 copy-done.2
  4.3 0.0 copy-done.3
  4.4 0.1 pad_maximum_fusion.2
  4.5 0.2 broadcast_in_dim.25
  4.8 0.5 tile.8
  5.3 0.3 pad_maximum_fusion
  5.6 54.5 %all_to_all.10.moved = bf16[128,104,128]{2,1,0:T(8,128)(2,1)S(1)} all-to-all(bf16[128,104,128]{2,1,0:T(8,128)(2,1)S(1)} %pad_maximum_fusion), channel_id=1, replica_groups=mesh['qrow'=32,'kcol'=4] {'qrow','kcol'}, dimensions={0} | all-to-all | bytes 6815744 | tf_op jit(solution)/shard_map/exchange_in/all_to_all | solution.py:311
  60.0 0.0 copy-start
  60.0 0.0 copy-start.7
  60.0 1.1 slice.26
  61.2 0.0 collective-permute-start
  61.2 0.0 copy-done.7
  61.2 0.1 select_reduce_fusion
  61.3 0.7 pad_add_fusion.table
  62.0 2.2 %collective-permute-done.other_half = bf16[128,32,128]{2,1,0:T(8,128)(2,1)} collective-permute-done((bf16[128,32,128]{2,1,0:T(8,128)(2,1)}, bf16[128,32,128]{2,1,0:T(8,128)(2,1)}, u32[]{:S(2)}, u32[]{:S(2)}) %collective-permute-start) | collective-permute-done | bytes 1048608 | tf_op jit(solution)/shard_map/exchange_in/ppermute | solution.py:312
  64.2 0.0 copy-done
  64.2 20.7 %softmax_totals.1.stats_0 = f32[16,512]{1,0:T(8,128)} custom-call(s32[131]{0:T(256)} %pad_add_fusion.table, bf16[128,104,128]{2,1,0:T(8,128)(2,1)} %copy-done, bf16[128,32,128]{2,1,0:T(8,128)(2,1)} %collective-permute-done.other_half), custom_call_target="tpu_custom_call" | custom-call | flops 2415919104 | bytes 4194304 | tf_op jit(solution)/shard_map/totals/softmax_totals/pallas_call | solution.py:228
  84.9 1.8 %collective-permute-start.3 = (f32[16,512]{1,0:T(8,128)}, f32[16,512]{1,0:T(8,128)S(1)}, u32[]{:S(2)}, u32[]{:S(2)}) collective-permute-start(f32[16,512]{1,0:T(8,128)} %softmax_totals.1.stats_0), channel_id=1, source_target_pairs={{0,96},{1,97},{2,98},{3,99},{4,100},{5,101},{6,102},{7,103},{8,104... | collective-permute-start | bytes 98312 | tf_op jit(solution)/shard_map/totals/ppermute | solution.py:323
  86.7 1.0 collective-permute-start.2
  87.7 0.8 collective-permute-start.1
  88.5 0.6 fusion.delta
  89.2 0.0 collective-permute-done.3.stats_3
  89.2 0.0 copy-start.4
  89.2 3.2 %collective-permute-done.2.stats_2 = f32[16,512]{1,0:T(8,128)S(1)} collective-permute-done((f32[16,512]{1,0:T(8,128)}, f32[16,512]{1,0:T(8,128)S(1)}, u32[]{:S(2)}, u32[]{:S(2)}) %collective-permute-start.2) | collective-permute-done | bytes 32800 | tf_op jit(solution)/shard_map/totals/ppermute | solution.py:323
  92.3 0.7 collective-permute-done.1.stats_1
  93.1 0.0 copy-done.4
  93.1 0.0 copy-done.5
  93.1 0.6 copy-done.6
  93.7 38.3 %gradients.1 = (bf16[128,32,128]{2,1,0:T(8,128)(2,1)}, bf16[128,32,128]{2,1,0:T(8,128)(2,1)}, bf16[128,32,128]{2,1,0:T(8,128)(2,1)}) custom-call(s32[131]{0:T(256)} %pad_add_fusion.table, bf16[128,104,128]{2,1,0:T(8,128)(2,1)} %copy-done, bf16[128,32,128]{2,1,0:T(8,128)(2,1)} %collective-permute-done.other_half, f32[128,128]{1,0:T(8,128)} %fusion.delta, ...), custom_call_target="tpu_custom_call" | custom-call | flops 12079595520 | bytes 8388608 | tf_op jit(solution)/shard_map/gradients/gradients/pallas_call | solution.py:249
  132.0 0.0 collective-permute-start.4
  132.0 2.9 %collective-permute-done.4 = bf16[128,32,128]{2,1,0:T(8,128)(2,1)S(1)} collective-permute-done((bf16[128,32,128]{2,1,0:T(8,128)(2,1)}, bf16[128,32,128]{2,1,0:T(8,128)(2,1)S(1)}, u32[]{:S(2)}, u32[]{:S(2)}) %collective-permute-start.4) | collective-permute-done | bytes 1048608 | tf_op jit(solution)/shard_map/exchange_out/ppermute | solution.py:329
  134.9 1.5 add_convert_fusion
  136.4 0.0 copy-done.1
  136.4 0.3 pad_maximum_fusion.1
  136.7 34.2 %all_to_all.11 = bf16[128,64,128]{2,1,0:T(8,128)(2,1)S(1)} all-to-all(bf16[128,64,128]{2,1,0:T(8,128)(2,1)S(1)} %pad_maximum_fusion.1), channel_id=1, replica_groups=mesh['qrow'=32,'kcol'=4] {'qrow','kcol'}, dimensions={0} | all-to-all | bytes 4194304 | tf_op jit(solution)/shard_map/exchange_out/all_to_all | solution.py:333
  170.9 1.9 %fusion.1 = (f32[128,32,128]{2,1,0:T(8,128)}, f32[128,32,128]{2,1,0:T(8,128)S(1)}) fusion(bf16[128,64,128]{2,1,0:T(8,128)(2,1)S(1)} %all_to_all.11), kind=kLoop, calls=%fused_computation.11 | loop fusion | bytes 8388608 | tf_op jit(solution)/shard_map/sums/slice | solution.py:345
  172.7 1.8 %reduce_sum.39 = bf16[4,2,2,16,128]{4,3,2,1,0:T(8,128)(2,1)S(1)} reduce(f32[4,16,2,2,16,128]{5,4,3,2,1,0:T(8,128)} %bitcast.24, f32[]{:T(128)} %constant.49.clone.1), dimensions={1}, to_apply=%region_3.4 | reduce | flops 491520 | bytes 2162692 | tf_op jit(solution)/shard_map/sums/reduce_sum | solution.py:344
  174.5 0.2 reduce_sum.38
  174.8 0.8 convert_element_type.63
  175.6 0.6 fusion.2
  (7 shorter events, 0.1 us)
Async XLA Ops:
  0.6 3.7 %copy-start.2 = (bf16[128,128]{1,0:T(8,128)(2,1)S(1)}, bf16[128,128]{1,0:T(8,128)(2,1)}, u32[]{:S(2)}) copy-start(bf16[128,128]{1,0:T(8,128)(2,1)} %param.8) | copy-start | bytes 98308
  0.6 3.7 %copy-start.3 = (bf16[128,128]{1,0:T(8,128)(2,1)S(1)}, bf16[128,128]{1,0:T(8,128)(2,1)}, u32[]{:S(2)}) copy-start(bf16[128,128]{1,0:T(8,128)(2,1)} %param.7) | copy-start | bytes 98308
  60.0 4.2 %copy-start = (bf16[128,104,128]{2,1,0:T(8,128)(2,1)}, bf16[128,104,128]{2,1,0:T(8,128)(2,1)S(1)}, u32[]{:S(2)}) copy-start(bf16[128,104,128]{2,1,0:T(8,128)(2,1)S(1)} %all_to_all.10.moved) | copy-start | bytes 10223620
  60.0 1.2 copy-start.7
  61.2 3.0 %collective-permute-start = (bf16[128,32,128]{2,1,0:T(8,128)(2,1)}, bf16[128,32,128]{2,1,0:T(8,128)(2,1)}, u32[]{:S(2)}, u32[]{:S(2)}) collective-permute-start(bf16[128,32,128]{2,1,0:T(8,128)(2,1)} %slice.26), channel_id=1, source_target_pairs={{0,1},{1,0},{2,3},{3,2},{4,5},{5,4},{6,7},{7,6},{8,9},{9,8},{10,11... | collective-permute-start | bytes 3145736 | tf_op jit(solution)/shard_map/exchange_in/ppermute | solution.py:312
  84.9 4.3 %collective-permute-start.3 = (f32[16,512]{1,0:T(8,128)}, f32[16,512]{1,0:T(8,128)S(1)}, u32[]{:S(2)}, u32[]{:S(2)}) collective-permute-start(f32[16,512]{1,0:T(8,128)} %softmax_totals.1.stats_0), channel_id=1, source_target_pairs={{0,96},{1,97},{2,98},{3,99},{4,100},{5,101},{6,102},{7,103},{8,104... | collective-permute-start | bytes 98312 | tf_op jit(solution)/shard_map/totals/ppermute | solution.py:323
  86.7 5.6 %collective-permute-start.2 = (f32[16,512]{1,0:T(8,128)}, f32[16,512]{1,0:T(8,128)S(1)}, u32[]{:S(2)}, u32[]{:S(2)}) collective-permute-start(f32[16,512]{1,0:T(8,128)} %softmax_totals.1.stats_0), channel_id=1, source_target_pairs={{0,64},{1,65},{2,66},{3,67},{4,68},{5,69},{6,70},{7,71},{8,72},{9,... | collective-permute-start | bytes 98312 | tf_op jit(solution)/shard_map/totals/ppermute | solution.py:323
  87.7 5.3 %collective-permute-start.1 = (f32[16,512]{1,0:T(8,128)}, f32[16,512]{1,0:T(8,128)S(1)}, u32[]{:S(2)}, u32[]{:S(2)}) collective-permute-start(f32[16,512]{1,0:T(8,128)} %softmax_totals.1.stats_0), channel_id=1, source_target_pairs={{0,32},{1,33},{2,34},{3,35},{4,36},{5,37},{6,38},{7,39},{8,40},{9,... | collective-permute-start | bytes 98312 | tf_op jit(solution)/shard_map/totals/ppermute | solution.py:323
  89.2 3.9 %copy-start.4 = (f32[16,512]{1,0:T(8,128)}, f32[16,512]{1,0:T(8,128)S(1)}, u32[]{:S(2)}) copy-start(f32[16,512]{1,0:T(8,128)S(1)} %collective-permute-done.3.stats_3) | copy-start | bytes 98308
  92.3 0.7 copy-start.5
  93.1 0.6 copy-start.6
  132.0 4.4 %copy-start.1 = (bf16[128,32,128]{2,1,0:T(8,128)(2,1)S(1)}, bf16[128,32,128]{2,1,0:T(8,128)(2,1)}, u32[]{:S(2)}) copy-start(bf16[128,32,128]{2,1,0:T(8,128)(2,1)} %get-tuple-element.6) | copy-start | bytes 3145732
  132.0 2.9 %collective-permute-start.4 = (bf16[128,32,128]{2,1,0:T(8,128)(2,1)}, bf16[128,32,128]{2,1,0:T(8,128)(2,1)S(1)}, u32[]{:S(2)}, u32[]{:S(2)}) collective-permute-start(bf16[128,32,128]{2,1,0:T(8,128)(2,1)} %get-tuple-element.8), channel_id=1, source_target_pairs={{0,1},{1,0},{2,3},{3,2},{4,5},{5,4},{6,7},{7,6},{8,9},{9,8},{10,11... | collective-permute-start | bytes 3145736 | tf_op jit(solution)/shard_map/exchange_out/ppermute | solution.py:329

commit v2 on v1

v2 whole, which is shorter than its diff:
```python
import jax
import jax.numpy as jnp
from jax import lax
from jax.experimental import pallas as pl
from jax.experimental.pallas import tpu as pltpu
from jax.sharding import PartitionSpec as P

ALL = ("qrow", "kcol")
DEVICES = 128
HEADS = 8
WIDTH = 128
STRETCH = 128
PLACES = 128
KEY_GROUPS = 4
ROW_GROUPS = 32
QUERY_TOKENS = 16
TOKEN_GROUPS = STRETCH // QUERY_TOKENS
PAIR = 2
HEAD_GROUPS = HEADS // PAIR
KEY_TOKENS = STRETCH // KEY_GROUPS
HALF = KEY_TOKENS // 2
ROWS = QUERY_TOKENS * PAIR
ALL_ROWS = PLACES * ROWS
ALL_KEYS = PLACES * KEY_TOKENS
TILE = 512
TILES = ALL_ROWS // TILE
SPAN = TILE // ROWS
SUBLANES = 8
BIG = 4096
WIDE = 512
BLOCK = 512
SKEW = 2
PART = 512
PARTS = 2 * TILE // PART
CHUNK = 128
NEGATIVE = -1e30
SCALE = float(WIDTH) ** (-0.5)
TO_LOG2 = SCALE * 1.4426950408889634
VMEM = 56 * 1024 * 1024


def contract(left, right, left_dim, right_dim):
    return lax.dot_general(
        left, right, (((left_dim,), (right_dim,)), ((), ())), preferred_element_type=jnp.float32
    )


def tile_at(index):
    return pl.ds(pl.multiple_of(index * TILE, TILE), TILE)


def allowed_on_diagonal(key_group, row_group, row_dim):
    row = lax.broadcasted_iota(jnp.int32, (TILE, TILE), row_dim)
    column = lax.broadcasted_iota(jnp.int32, (TILE, TILE), 1 - row_dim)
    first_token = (row_group // HEAD_GROUPS) * QUERY_TOKENS
    row_place = (row // ROWS) * STRETCH + first_token + row % QUERY_TOKENS
    key_place = (column // KEY_TOKENS) * STRETCH + key_group * KEY_TOKENS + column % KEY_TOKENS
    return key_place <= row_place


def stats_kernel(table, scored, other_key, stats, query, key):
    key_group, row_group, core = table[PLACES], table[PLACES + 1], table[PLACES + 2]

    def sort(place, carry):
        source = table[place]
        query[pl.ds(pl.multiple_of(place * ROWS, ROWS), ROWS)] = scored[source, 0:ROWS]
        first = pl.multiple_of(place * KEY_TOKENS + core * HALF, HALF)
        second = pl.multiple_of(place * KEY_TOKENS + (1 - core) * HALF, HALF)
        key[pl.ds(first, HALF)] = scored[source, ROWS : ROWS + HALF]
        key[pl.ds(second, HALF)] = other_key[source]
        return carry

    lax.fori_loop(0, PLACES, sort, 0, unroll=8)

    def absorb(keys, rows, state, allowed):
        scores = contract(keys, rows, 1, 1)
        if allowed is not None:
            scores = jnp.where(allowed, scores, NEGATIVE)
        highest, summed = state
        scores = scores.reshape(keys.shape[0] // SUBLANES, SUBLANES, rows.shape[0])
        raised = jnp.maximum(highest, jnp.max(scores, axis=0))
        summed = summed * jnp.exp2((highest - raised) * TO_LOG2)
        return raised, summed + jnp.sum(jnp.exp2((scores - raised[None]) * TO_LOG2), axis=0)

    allowed = allowed_on_diagonal(key_group, row_group, 1)
    def per_row_pair(i, carry):
        rows = [
            query[pl.ds(pl.multiple_of(i * 2 * TILE + k * PART, PART), PART)] for k in range(PARTS)
        ]

        def keys_at(j, n):
            return key[pl.ds(pl.multiple_of(j * TILE + n * CHUNK, CHUNK), CHUNK)]

        def full_tile(j, state):
            state = list(state)
            for n in range(TILE // CHUNK):
                keys = keys_at(j, n)
                for k in range(PARTS):
                    state[k] = absorb(keys, rows[k], state[k], None)
            return tuple(state)

        start = (
            jnp.full((SUBLANES, PART), NEGATIVE, jnp.float32),
            jnp.zeros((SUBLANES, PART), jnp.float32),
        )
        state = list(lax.fori_loop(0, 2 * i, full_tile, (start,) * PARTS))
        for n in range(TILE // CHUNK):
            keys = keys_at(2 * i, n)
            for k in range(PARTS):
                mask = None
                if k < PARTS // 2:
                    mask = allowed[n * CHUNK : (n + 1) * CHUNK, k * PART : (k + 1) * PART]
                state[k] = absorb(keys, rows[k], state[k], mask)
            keys = keys_at(2 * i + 1, n)
            for k in range(PARTS // 2):
                mask = allowed[n * CHUNK : (n + 1) * CHUNK, k * PART : (k + 1) * PART]
                late = k + PARTS // 2
                state[late] = absorb(keys, rows[late], state[late], mask)
        for k in range(PARTS):
            highest, summed = state[k]
            row_peak = jnp.max(highest, axis=0, keepdims=True)
            row_total = jnp.sum(
                summed * jnp.exp2((highest - row_peak) * TO_LOG2), axis=0, keepdims=True
            )
            tile = 2 * i + k // (PARTS // 2)
            lanes = (k % (PARTS // 2)) * PART
            stats[pl.ds(tile, 1), lanes : lanes + PART] = row_peak
            stats[pl.ds(tile + TILES, 1), lanes : lanes + PART] = row_total
        return carry

    lax.fori_loop(0, TILES // 2, per_row_pair, 0)


def gradient_kernel(
    table,
    scored,
    other_key,
    weighed,
    other_value,
    delta,
    stats_0,
    stats_1,
    stats_2,
    stats_3,
    own_grad,
    other_grad,
    query,
    grad,
    key,
    value,
    query_turned,
    grad_turned,
    logs,
    query_total,
    key_total,
    value_total,
    key_sorted,
    value_sorted,
):
    key_group, row_group, core = table[PLACES], table[PLACES + 1], table[PLACES + 2]
    lane = lax.broadcasted_iota(jnp.int32, (TILE, WIDTH), 1)
    all_stats = [ref[...] for ref in (stats_0, stats_1, stats_2, stats_3)]
    peaks = [part[0:TILES] for part in all_stats]
    highest = jnp.maximum(jnp.maximum(peaks[0], peaks[1]), jnp.maximum(peaks[2], peaks[3]))
    summed = jnp.zeros_like(highest)
    for part in all_stats:
        summed = summed + part[TILES:] * jnp.exp2((part[0:TILES] - highest) * TO_LOG2)
    log_totals = highest + jnp.log2(summed) * (1.0 / TO_LOG2)
    high = log_totals.astype(jnp.bfloat16).astype(jnp.float32)
    middle = (log_totals - high).astype(jnp.bfloat16).astype(jnp.float32)
    low = (log_totals - high - middle).astype(jnp.bfloat16).astype(jnp.float32)
    padding = jnp.zeros((WIDTH - 3 * TILES, TILE), jnp.float32)
    logs[...] = jnp.concatenate([high, middle, low, padding], axis=0).T

    extra_lane = lax.broadcasted_iota(jnp.int32, (ALL_KEYS, WIDTH), 1)
    key[:, WIDTH:] = jnp.where(extra_lane < 3 * TILES, -1.0, 0.0).astype(jnp.bfloat16)
    value[:, WIDTH:] = jnp.where(extra_lane < ROWS, -1.0, 0.0).astype(jnp.bfloat16)
    row_sub = lax.broadcasted_iota(jnp.int32, (ROWS, WIDTH), 0)
    row_lane = lax.broadcasted_iota(jnp.int32, (ROWS, WIDTH), 1)

    def sort(place, carry):
        source = table[place]
        spot = pl.ds(pl.multiple_of(place * ROWS, ROWS), ROWS)
        query[spot, 0:WIDTH] = scored[source, 0:ROWS]
        grad[spot, 0:WIDTH] = weighed[source, 0:ROWS]
        grad[spot, WIDTH:] = jnp.where(
            row_sub == row_lane, jnp.broadcast_to(delta[pl.ds(source, 1)], (ROWS, WIDTH)), 0.0
        ).astype(jnp.bfloat16)
        first = pl.ds(pl.multiple_of(place * KEY_TOKENS + core * HALF, HALF), HALF)
        second = pl.ds(pl.multiple_of(place * KEY_TOKENS + (1 - core) * HALF, HALF), HALF)
        key[first, 0:WIDTH] = scored[source, ROWS : ROWS + HALF]
        key[second, 0:WIDTH] = other_key[source]
        value[first, 0:WIDTH] = weighed[source, ROWS : ROWS + HALF]
        value[second, 0:WIDTH] = other_value[source]
        return carry

    lax.fori_loop(0, PLACES, sort, 0, unroll=8)
    key_total[...] = jnp.zeros_like(key_total)
    value_total[...] = jnp.zeros_like(value_total)

    allowed = allowed_on_diagonal(key_group, row_group, 0)[0:BLOCK, 0:BLOCK]

    def per_row_tile(i, carry):
        chosen_lanes = lane < 3 * TILES
        for h in range(BIG // TILE):
            here = tile_at(i * (BIG // TILE) + h)
            chosen = jnp.logical_and(lane % TILES == i * (BIG // TILE) + h, chosen_lanes)
            query[here, WIDTH:] = jnp.where(chosen, logs[...], 0.0).astype(jnp.bfloat16)
            query_turned[:, h * TILE : (h + 1) * TILE] = query[here, 0:WIDTH].T
            grad_turned[:, h * TILE : (h + 1) * TILE] = grad[here, 0:WIDTH].T
        query_total[...] = jnp.zeros_like(query_total)

        def rows_at(r):
            return pl.ds(pl.multiple_of(i * BIG + r * BLOCK, BLOCK), BLOCK)

        def work(keys_at, blocks):
            def first(block):
                r, k, masked = block
                scores = contract(query[rows_at(r)], key[keys_at(k)], 1, 1)
                probs = jnp.exp2(scores * TO_LOG2)
                if masked:
                    probs = jnp.where(allowed, probs, 0.0)
                moved_probs = contract(grad[rows_at(r)], value[keys_at(k)], 1, 1)
                return probs.astype(jnp.bfloat16), (probs * moved_probs).astype(jnp.bfloat16)

            value_sums, key_sums, query_sums = {}, {}, {}

            def add(sums, spot, part):
                sums[spot] = sums[spot] + part if spot in sums else part

            def second(block, probs_low, dscores):
                r, k, _ = block
                span = slice(r * BLOCK, (r + 1) * BLOCK)
                add(value_sums, k, contract(grad_turned[:, span], probs_low, 1, 0))
                add(key_sums, k, contract(query_turned[:, span], dscores, 1, 0))
                add(query_sums, r, contract(dscores, key[keys_at(k), 0:WIDTH], 1, 0))

            waiting = []
            for block in blocks:
                waiting.append((block,) + first(block))
                if len(waiting) > SKEW:
                    second(*waiting.pop(0))
            for entry in waiting:
                second(*entry)
            for k, part in value_sums.items():
                value_total[:, keys_at(k)] += part
            for k, part in key_sums.items():
                key_total[:, keys_at(k)] += part
            for r, part in query_sums.items():
                query_total[r * BLOCK : (r + 1) * BLOCK] += part

        def full_tile(j, inner):
            def keys_at(k):
                return pl.ds(pl.multiple_of(j * WIDE + k * BLOCK, BLOCK), BLOCK)

            work(
                keys_at,
                [(r, k, False) for k in range(WIDE // BLOCK) for r in range(BIG // BLOCK)],
            )
            return inner

        lax.fori_loop(0, i * (BIG // WIDE), full_tile, 0)
        work(
            rows_at,
            [(r, k, r == k) for k in range(BIG // BLOCK) for r in range(k, BIG // BLOCK)],
        )

        for k in range(BIG // ROWS):
            source = table[i * (BIG // ROWS) + k]
            own_grad[source, 0:ROWS] = (query_total[k * ROWS : (k + 1) * ROWS] * SCALE).astype(
                jnp.bfloat16
            )
        return carry

    lax.fori_loop(0, ALL_ROWS // BIG, per_row_tile, 0)

    def turn(j, carry):
        there = tile_at(j)
        key_sorted[there] = key_total[:, there].T * SCALE
        value_sorted[there] = value_total[:, there].T
        return carry

    lax.fori_loop(0, TILES, turn, 0)

    def unsort(place, carry):
        source = table[place]
        first = pl.ds(pl.multiple_of(place * KEY_TOKENS + core * HALF, HALF), HALF)
        second = pl.ds(pl.multiple_of(place * KEY_TOKENS + (1 - core) * HALF, HALF), HALF)
        own_grad[source, ROWS : ROWS + HALF] = key_sorted[first].astype(jnp.bfloat16)
        own_grad[source, ROWS + HALF :] = value_sorted[first].astype(jnp.bfloat16)
        other_grad[source, 0:HALF] = key_sorted[second].astype(jnp.bfloat16)
        other_grad[source, HALF:] = value_sorted[second].astype(jnp.bfloat16)
        return carry

    lax.fori_loop(0, PLACES, unsort, 0, unroll=8)


IN_VMEM = pl.BlockSpec(memory_space=pltpu.VMEM)
IN_SMEM = pl.BlockSpec(memory_space=pltpu.SMEM)
PAIRS = TILE * TILE * TILES * (TILES + 1) // 2


def stats_call(table, scored, other_key):
    return pl.pallas_call(
        stats_kernel,
        out_shape=jax.ShapeDtypeStruct((2 * TILES, TILE), jnp.float32),
        in_specs=[IN_SMEM, IN_VMEM, IN_VMEM],
        out_specs=IN_VMEM,
        scratch_shapes=[
            pltpu.VMEM((ALL_ROWS, WIDTH), jnp.bfloat16),
            pltpu.VMEM((ALL_KEYS, WIDTH), jnp.bfloat16),
        ],
        compiler_params=pltpu.CompilerParams(vmem_limit_bytes=VMEM),
        cost_estimate=pl.CostEstimate(
            flops=2 * PAIRS * WIDTH, bytes_accessed=4 << 20, transcendentals=PAIRS
        ),
        name="softmax_totals",
    )(table, scored, other_key)


def gradient_call(table, scored, other_key, weighed, other_value, delta, stats):
    own = jax.ShapeDtypeStruct((PLACES, ROWS + 2 * HALF, WIDTH), jnp.bfloat16)
    other = jax.ShapeDtypeStruct((PLACES, 2 * HALF, WIDTH), jnp.bfloat16)
    return pl.pallas_call(
        gradient_kernel,
        out_shape=(own, other),
        in_specs=[IN_SMEM] + [IN_VMEM] * 9,
        out_specs=(IN_VMEM,) * 2,
        scratch_shapes=[
            pltpu.VMEM((ALL_ROWS, 2 * WIDTH), jnp.bfloat16),
            pltpu.VMEM((ALL_ROWS, 2 * WIDTH), jnp.bfloat16),
            pltpu.VMEM((ALL_KEYS, 2 * WIDTH), jnp.bfloat16),
            pltpu.VMEM((ALL_KEYS, 2 * WIDTH), jnp.bfloat16),
            pltpu.VMEM((WIDTH, BIG), jnp.bfloat16),
            pltpu.VMEM((WIDTH, BIG), jnp.bfloat16),
            pltpu.VMEM((TILE, WIDTH), jnp.float32),
            pltpu.VMEM((BIG, WIDTH), jnp.float32),
            pltpu.VMEM((WIDTH, ALL_KEYS), jnp.float32),
            pltpu.VMEM((WIDTH, ALL_KEYS), jnp.float32),
            pltpu.VMEM((ALL_KEYS, WIDTH), jnp.float32),
            pltpu.VMEM((ALL_KEYS, WIDTH), jnp.float32),
        ],
        compiler_params=pltpu.CompilerParams(vmem_limit_bytes=VMEM),
        cost_estimate=pl.CostEstimate(
            flops=10 * PAIRS * WIDTH, bytes_accessed=8 << 20, transcendentals=PAIRS
        ),
        name="gradients",
    )(table, scored, other_key, weighed, other_value, delta, *stats)


def pack_kernel(rows, keys, outgoing):
    for r in range(ROW_GROUPS):
        tokens = (r // HEAD_GROUPS) * QUERY_TOKENS
        for h in range(PAIR):
            head = (r % HEAD_GROUPS) * PAIR + h
            part = rows[tokens : tokens + QUERY_TOKENS, head * WIDTH : (head + 1) * WIDTH]
            for g in range(KEY_GROUPS):
                outgoing[
                    g * ROW_GROUPS + r, h * QUERY_TOKENS : (h + 1) * QUERY_TOKENS
                ] = part
    for g in range(KEY_GROUPS):
        for c in range(2):
            first = g * KEY_TOKENS + c * HALF
            part = keys[first : first + HALF]
            for r in range(c, ROW_GROUPS, 2):
                outgoing[g * ROW_GROUPS + r, ROWS : ROWS + HALF] = part


def pack_call(rows, keys):
    return pl.pallas_call(
        pack_kernel,
        out_shape=jax.ShapeDtypeStruct((DEVICES, ROWS + HALF, WIDTH), jnp.bfloat16),
        in_specs=[IN_VMEM] * 2,
        out_specs=IN_VMEM,
        compiler_params=pltpu.CompilerParams(vmem_limit_bytes=VMEM // 4),
        name="pack",
    )(rows, keys)


def pair_kernel(own, received, outgoing):
    outgoing[:, 0:ROWS] = own[:, 0:ROWS]
    total = own[:, ROWS:].astype(jnp.float32) + received[...].astype(jnp.float32)
    outgoing[:, ROWS:] = total.astype(jnp.bfloat16)


def pair_call(own, received):
    return pl.pallas_call(
        pair_kernel,
        out_shape=jax.ShapeDtypeStruct(own.shape, own.dtype),
        in_specs=[IN_VMEM] * 2,
        out_specs=IN_VMEM,
        compiler_params=pltpu.CompilerParams(vmem_limit_bytes=VMEM // 2),
        name="pair_sum",
    )(own, received)


def sums_kernel(back, d_query, d_key, d_value):
    for r in range(ROW_GROUPS):
        total = back[r, 0:ROWS].astype(jnp.float32)
        for g in range(1, KEY_GROUPS):
            total = total + back[g * ROW_GROUPS + r, 0:ROWS].astype(jnp.float32)
        total = total.astype(jnp.bfloat16)
        tokens = (r // HEAD_GROUPS) * QUERY_TOKENS
        for h in range(PAIR):
            head = (r % HEAD_GROUPS) * PAIR + h
            d_query[tokens : tokens + QUERY_TOKENS, head * WIDTH : (head + 1) * WIDTH] = total[
                h * QUERY_TOKENS : (h + 1) * QUERY_TOKENS
            ]
    for g in range(KEY_GROUPS):
        for c in range(2):
            total = jnp.zeros((2 * HALF, WIDTH), jnp.float32)
            for r in range(c, ROW_GROUPS, 2):
                total = total + back[g * ROW_GROUPS + r, ROWS:].astype(jnp.float32)
            first = g * KEY_TOKENS + c * HALF
            d_key[first : first + HALF] = total[0:HALF].astype(jnp.bfloat16)
            d_value[first : first + HALF] = total[HALF:].astype(jnp.bfloat16)


def sums_call(back):
    small = jax.ShapeDtypeStruct((STRETCH, WIDTH), jnp.bfloat16)
    return pl.pallas_call(
        sums_kernel,
        out_shape=(
            jax.ShapeDtypeStruct((STRETCH, HEADS * WIDTH), jnp.bfloat16),
            small,
            small,
        ),
        in_specs=[IN_VMEM],
        out_specs=(IN_VMEM,) * 3,
        compiler_params=pltpu.CompilerParams(vmem_limit_bytes=VMEM // 4),
        name="sums",
    )(back)


def shards(queries, key_states, value_states, out_grad, forward_out, stretch_order):
    me = lax.axis_index(ALL)
    swap = [(d, d ^ 1) for d in range(DEVICES)]

    def around(step):
        return [(d, (d + step * ROW_GROUPS) % DEVICES) for d in range(DEVICES)]

    with jax.named_scope("outgoing"):
        scored = pack_call(queries, key_states)
        products = out_grad.astype(jnp.float32) * forward_out.astype(jnp.float32)
        delta = jnp.sum(products.reshape(STRETCH, HEADS, WIDTH), axis=2).astype(jnp.bfloat16)
        delta = delta.reshape(TOKEN_GROUPS, QUERY_TOKENS, HEAD_GROUPS, PAIR)
        delta = delta.transpose(0, 2, 3, 1).reshape(ROW_GROUPS, 1, ROWS)
        delta = jnp.pad(delta, ((0, 0), (0, 7), (0, WIDTH - ROWS)))
        weighed = jnp.concatenate(
            [pack_call(out_grad, value_states), jnp.tile(delta, (KEY_GROUPS, 1, 1))], axis=1
        )
    with jax.named_scope("table"):
        places = jnp.arange(PLACES, dtype=jnp.int32)
        holder = jnp.sum(
            jnp.where(stretch_order[None, :] == places[:, None], places[None, :], 0), axis=1
        )
        ids = jnp.stack([me // ROW_GROUPS, me % ROW_GROUPS, me % 2]).astype(jnp.int32)
        table = jnp.concatenate([holder, ids])
    with jax.named_scope("exchange_in"):
        scored = lax.all_to_all(scored, ALL, split_axis=0, concat_axis=0, tiled=True)
        weighed = lax.all_to_all(weighed, ALL, split_axis=0, concat_axis=0, tiled=True)
        other_key = lax.ppermute(scored[:, ROWS:], ALL, swap)
    with jax.named_scope("totals"):
        stats = stats_call(table, scored, other_key)
        all_stats = [stats] + [lax.ppermute(stats, ALL, around(k)) for k in range(1, KEY_GROUPS)]
        weighed, *all_stats = lax.optimization_barrier((weighed, *all_stats))
        other_value = lax.ppermute(weighed[:, ROWS : ROWS + HALF], ALL, swap)
        delta_in = weighed[:, ROWS + HALF, :].astype(jnp.float32)
    with jax.named_scope("gradients"):
        own_grad, other_grad = gradient_call(
            table, scored, other_key, weighed, other_value, delta_in, all_stats
        )
    with jax.named_scope("exchange_out"):
        received = lax.ppermute(other_grad, ALL, swap)
        outgoing = pair_call(own_grad, received)
        back = lax.all_to_all(outgoing, ALL, split_axis=0, concat_axis=0, tiled=True)
    with jax.named_scope("sums"):
        return sums_call(back)


def solution(mesh):
    split = P(ALL, None)
    return jax.shard_map(
        shards,
        mesh=mesh,
        in_specs=(split,) * 5 + (P(),),
        out_specs=(split,) * 3,
        check_vma=False,
    )
```

time: 177 us -> 146 us (0.82)
  blocking collectives: 88.6 us -> 36.9 us
  waiting for transfers between devices: 8.94 us -> 32.3 us
  starting transfers between devices: 3.62 us -> 19.8 us
  Pallas kernels: 59 us -> 46.2 us
  other arithmetic: 6.93 us -> 3.18 us
    all_to_all x1 -> x0, blocking collectives: 34.2 us -> none  [shards(): lax.all_to_all(jnp.concatenate([query_grad, pair_grad], axis=1), ALL, spl...]
    all_to_all x0 -> x2, waiting for transfers between devices: none -> 27.9 us  [the longest x1 21.9 us: shards(): lax.all_to_all(scored, ALL, split_axis=0, concat_axis=0, tiled=True)]
    all_to_all x1, blocking collectives: 54.5 us -> 36.9 us  [shards(): lax.all_to_all(outgoing, ALL, split_axis=0, concat_axis=0, tiled=True)]
    all_to_all x0 -> x2, starting transfers between devices: none -> 15.8 us  [the longest x1 11.1 us: shards(): lax.all_to_all(scored, ALL, split_axis=0, concat_axis=0, tiled=True)]
    pallas_call x1, Pallas kernels: 20.7 us -> 14.2 us  [stats_call(): pl.pallas_call(stats_kernel, out_shape=jax.ShapeDtypeStruct((2 * TILES, T...]
    pallas_call x1 -> x5, Pallas kernels: 38.3 us -> 32 us  [the longest x1 29.2 us: gradient_call(): pl.pallas_call(gradient_kernel, out_shape=(own, other), in_specs=[IN_SMEM...]
    unnamed x17 -> x27, local copies, waits for them, and re-layouts: 0.74 us -> 4.87 us
    ppermute x3, waiting for transfers between devices: 3.89 us -> 0.01 us  [shards(): lax.ppermute(stats, ALL, around(k))]
  transfers between devices with their start and end apart: 5 -> 8, of which waited for: 4 -> 5; matrix products, arithmetic and copies ran while one was open for 1% -> 3% of each run, Pallas kernels for 0% -> 10%
where the time goes in v2:
time: 146 us
  Pallas kernels  46.2 us (32%)
  blocking collectives  36.9 us (25%)
  waiting for transfers between devices  32.3 us (22%)
  starting transfers between devices  19.8 us (14%)
  local copies, waits for them, and re-layouts  6.52 us (4%)
  other arithmetic  3.18 us (2%)
    all_to_all x1, blocking collectives, shards(): lax.all_to_all(outgoing, ALL, split_axis=0, concat_axis=0, tiled=True)  36.9 us
    pallas_call x1, Pallas kernels, gradient_call(): pl.pallas_call(gradient_kernel, out_shape=(own, other), in_specs=[IN_SMEM...  29.2 us
    all_to_all x1, waiting for transfers between devices, shards(): lax.all_to_all(scored, ALL, split_axis=0, concat_axis=0, tiled=True)  21.9 us
    pallas_call x1, Pallas kernels, stats_call(): pl.pallas_call(stats_kernel, out_shape=jax.ShapeDtypeStruct((2 * TILES, T...  14.2 us
    all_to_all x1, starting transfers between devices, shards(): lax.all_to_all(scored, ALL, split_axis=0, concat_axis=0, tiled=True)  11.1 us
    all_to_all x1, waiting for transfers between devices, shards(): lax.all_to_all(weighed, ALL, split_axis=0, concat_axis=0, tiled=True)  5.97 us
    unnamed x27, local copies, waits for them, and re-layouts  4.87 us
    all_to_all x1, starting transfers between devices, shards(): lax.all_to_all(weighed, ALL, split_axis=0, concat_axis=0, tiled=True)  4.64 us
  transfers between devices with their start and end apart: 8, of which 5 were waited for; matrix products, arithmetic and copies ran while one was open for 3% of the time, Pallas kernels for 10%

profile of v2, /device:TPU:0, one launch (start us, length us, event | category | flops | bytes accessed | tf_op | source)
XLA Modules:
  0.0 145.6 jit_solution(3871121396752404421)
XLA Ops:
  0.6 0.0 copy-start.2
  0.6 0.9 copy-done.2
  1.6 0.8 copy-done.3
  2.3 1.4 pack.2
  3.7 11.1 %all-to-all-start = ((bf16[128,48,128]{2,1,0:T(8,128)(2,1)}), bf16[128,48,128]{2,1,0:T(8,128)(2,1)S(1)}, u32[]{:S(2)}, u32[]{:S(2)}) async-start(bf16[128,48,128]{2,1,0:T(8,128)(2,1)} %pack.2), calls=%async_computation | async-start | bytes 3145728 | tf_op jit(solution)/shard_map/exchange_in/all_to_all | solution.py:460
  14.8 0.0 copy-done.1
  14.9 0.0 copy-done.7
  14.9 0.0 copy-start.4
  14.9 0.1 multiply_bitcast_fusion
  14.9 0.1 copy.32
  15.1 0.2 reduce_sum.19
  15.3 0.1 copy.27
  15.4 0.1 convert_element_type.23
  15.5 0.1 reshape.25
  15.6 0.1 copy-done.4
  15.6 0.2 pack.3
  15.9 1.5 %pad_maximum_fusion = bf16[128,56,128]{2,1,0:T(8,128)(2,1)} fusion(bf16[128,8,128]{2,1,0:T(8,128)(2,1)S(1)} %bitcast.16, bf16[128,48,128]{2,1,0:T(8,128)(2,1)S(1)} %pack.3), kind=kLoop, calls=%fused_computation | loop fusion | flops 3670016 | bytes 3670016 | tf_op jit(solution)/shard_map/outgoing/concatenate | solution.py:449
  17.4 21.9 %all-to-all-done.scored = bf16[128,48,128]{2,1,0:T(8,128)(2,1)S(1)} async-done(((bf16[128,48,128]{2,1,0:T(8,128)(2,1)}), bf16[128,48,128]{2,1,0:T(8,128)(2,1)S(1)}, u32[]{:S(2)}, u32[]{:S(2)}) %all-to-all-start) | async-done | bytes 1572896 | tf_op jit(solution)/shard_map/exchange_in/all_to_all | solution.py:460
  39.3 4.6 %all-to-all-start.1 = ((bf16[128,56,128]{2,1,0:T(8,128)(2,1)}), bf16[128,56,128]{2,1,0:T(8,128)(2,1)S(1)}, u32[]{:S(2)}, u32[]{:S(2)}) async-start(bf16[128,56,128]{2,1,0:T(8,128)(2,1)} %pad_maximum_fusion), calls=%async_computation.1 | async-start | bytes 3670016 | tf_op jit(solution)/shard_map/exchange_in/all_to_all | solution.py:461
  43.9 0.8 slice.12
  44.8 0.0 collective-permute-start
  44.8 0.1 select_reduce_fusion
  44.9 0.7 pad_add_fusion.table
  45.6 1.5 collective-permute-done.other_key
  47.0 14.2 %softmax_totals.1.stats_0 = f32[16,512]{1,0:T(8,128)} custom-call(s32[131]{0:T(256)} %pad_add_fusion.table, bf16[128,48,128]{2,1,0:T(8,128)(2,1)} %copy-done.6, bf16[128,16,128]{2,1,0:T(8,128)(2,1)} %collective-permute-done.other_key), custom_call_target="tpu_custom_call" | custom-call | flops 2415919104 | bytes 4194304 | tf_op jit(solution)/shard_map/totals/softmax_totals/pallas_call | solution.py:304
  61.3 2.1 %collective-permute-start.3 = (f32[16,512]{1,0:T(8,128)}, f32[16,512]{1,0:T(8,128)S(1)}, u32[]{:S(2)}, u32[]{:S(2)}) collective-permute-start(f32[16,512]{1,0:T(8,128)} %softmax_totals.1.stats_0), channel_id=1, source_target_pairs={{0,96},{1,97},{2,98},{3,99},{4,100},{5,101},{6,102},{7,103},{8,104... | collective-permute-start | bytes 98312 | tf_op jit(solution)/shard_map/totals/ppermute | solution.py:465
  63.3 0.8 collective-permute-start.2
  64.2 0.9 collective-permute-start.1
  65.0 6.0 %all-to-all-done.1.weighed = bf16[128,56,128]{2,1,0:T(8,128)(2,1)S(1)} async-done(((bf16[128,56,128]{2,1,0:T(8,128)(2,1)}), bf16[128,56,128]{2,1,0:T(8,128)(2,1)S(1)}, u32[]{:S(2)}, u32[]{:S(2)}) %all-to-all-start.1) | async-done | bytes 1835040 | tf_op jit(solution)/shard_map/exchange_in/all_to_all | solution.py:461
  71.0 0.0 collective-permute-done.3.stats_3
  71.0 0.0 collective-permute-done.2.stats_2
  71.0 0.0 collective-permute-done.1.stats_1
  71.1 0.0 copy-start.11
  71.1 0.1 collective-permute-start.4
  71.2 0.4 copy.30
  71.7 0.6 copy-done.5
  72.3 0.0 copy-done.9
  72.3 0.0 copy-done.10
  72.3 0.6 fusion.delta
  72.9 0.2 collective-permute-done.4.other_value
  73.1 0.8 copy-done.8
  73.9 29.2 %gradients.1 = (bf16[128,64,128]{2,1,0:T(8,128)(2,1)}, bf16[128,32,128]{2,1,0:T(8,128)(2,1)}) custom-call(s32[131]{0:T(256)} %pad_add_fusion.table, bf16[128,48,128]{2,1,0:T(8,128)(2,1)} %copy-done.6, bf16[128,16,128]{2,1,0:T(8,128)(2,1)} %collective-permute-done.other_key, bf16[128,56,128]{2,1,0:T(8,128)(2,1)} %copy-done.5, ...), custom_call_target="tpu_custom_call" | custom-call | flops 12079595520 | bytes 8388608 | tf_op jit(solution)/shard_map/gradients/gradients/pallas_call | solution.py:324
  103.1 0.1 collective-permute-start.5
  103.2 2.7 %collective-permute-done.5.received = bf16[128,32,128]{2,1,0:T(8,128)(2,1)S(1)} collective-permute-done((bf16[128,32,128]{2,1,0:T(8,128)(2,1)}, bf16[128,32,128]{2,1,0:T(8,128)(2,1)S(1)}, u32[]{:S(2)}, u32[]{:S(2)}) %collective-permute-start.5) | collective-permute-done | bytes 1048608 | tf_op jit(solution)/shard_map/exchange_out/ppermute | solution.py:474
  106.0 1.6 %copy-done = bf16[128,64,128]{2,1,0:T(8,128)(2,1)S(1)} copy-done((bf16[128,64,128]{2,1,0:T(8,128)(2,1)S(1)}, bf16[128,64,128]{2,1,0:T(8,128)(2,1)}, u32[]{:S(2)}) %copy-start) | copy-done | bytes 2097176
  107.5 0.3 pair_sum.1
  107.8 36.9 %all_to_all.15.back = bf16[128,64,128]{2,1,0:T(8,128)(2,1)S(1)} all-to-all(bf16[128,64,128]{2,1,0:T(8,128)(2,1)S(1)} %pair_sum.1), channel_id=1, replica_groups=mesh['qrow'=32,'kcol'=4] {'qrow','kcol'}, dimensions={0} | all-to-all | bytes 4194304 | tf_op jit(solution)/shard_map/exchange_out/all_to_all | solution.py:476
  144.7 0.9 sums.1
  (17 shorter events, 0.2 us)
Async XLA Ops:
  0.6 1.0 copy-start.2
  1.6 0.8 copy-start.3
  3.7 11.2 %copy-start.1 = (bf16[128,1024]{1,0:T(8,128)(2,1)S(1)}, bf16[128,1024]{1,0:T(8,128)(2,1)}, u32[]{:S(2)}) copy-start(bf16[128,1024]{1,0:T(8,128)(2,1)} %rows.3) | copy-start | bytes 786436
  3.7 11.2 %copy-start.7 = (bf16[128,1024]{1,0:T(8,128)(2,1)S(1)}, bf16[128,1024]{1,0:T(8,128)(2,1)}, u32[]{:S(2)}) copy-start(bf16[128,1024]{1,0:T(8,128)(2,1)} %param.10) | copy-start | bytes 786436
  3.7 35.6 %all-to-all-start = ((bf16[128,48,128]{2,1,0:T(8,128)(2,1)}), bf16[128,48,128]{2,1,0:T(8,128)(2,1)S(1)}, u32[]{:S(2)}, u32[]{:S(2)}) async-start(bf16[128,48,128]{2,1,0:T(8,128)(2,1)} %pack.2), calls=%async_computation | async-start | bytes 3145728 | tf_op jit(solution)/shard_map/exchange_in/all_to_all | solution.py:460
  14.9 0.8 copy-start.4
  17.4 27.4 %copy-start.12 = (s32[128]{0:T(128)S(1)}, s32[128]{0:T(128)}, u32[]{:S(2)}) copy-start(s32[128]{0:T(128)} %param.11) | copy-start | bytes 1540
  39.3 5.5 %copy-start.6 = (bf16[128,48,128]{2,1,0:T(8,128)(2,1)}, bf16[128,48,128]{2,1,0:T(8,128)(2,1)S(1)}, u32[]{:S(2)}) copy-start(bf16[128,48,128]{2,1,0:T(8,128)(2,1)S(1)} %all-to-all-done.scored) | copy-start | bytes 4718596
  39.3 31.7 %all-to-all-start.1 = ((bf16[128,56,128]{2,1,0:T(8,128)(2,1)}), bf16[128,56,128]{2,1,0:T(8,128)(2,1)S(1)}, u32[]{:S(2)}, u32[]{:S(2)}) async-start(bf16[128,56,128]{2,1,0:T(8,128)(2,1)} %pad_maximum_fusion), calls=%async_computation.1 | async-start | bytes 3670016 | tf_op jit(solution)/shard_map/exchange_in/all_to_all | solution.py:461
  44.8 2.3 %collective-permute-start = (bf16[128,16,128]{2,1,0:T(8,128)(2,1)}, bf16[128,16,128]{2,1,0:T(8,128)(2,1)}, u32[]{:S(2)}, u32[]{:S(2)}) collective-permute-start(bf16[128,16,128]{2,1,0:T(8,128)(2,1)} %slice.12), channel_id=1, source_target_pairs={{0,1},{1,0},{2,3},{3,2},{4,5},{5,4},{6,7},{7,6},{8,9},{9,8},{10,11... | collective-permute-start | bytes 1572872 | tf_op jit(solution)/shard_map/exchange_in/ppermute | solution.py:462
  61.3 9.7 %collective-permute-start.3 = (f32[16,512]{1,0:T(8,128)}, f32[16,512]{1,0:T(8,128)S(1)}, u32[]{:S(2)}, u32[]{:S(2)}) collective-permute-start(f32[16,512]{1,0:T(8,128)} %softmax_totals.1.stats_0), channel_id=1, source_target_pairs={{0,96},{1,97},{2,98},{3,99},{4,100},{5,101},{6,102},{7,103},{8,104... | collective-permute-start | bytes 98312 | tf_op jit(solution)/shard_map/totals/ppermute | solution.py:465
  63.3 7.7 %collective-permute-start.2 = (f32[16,512]{1,0:T(8,128)}, f32[16,512]{1,0:T(8,128)S(1)}, u32[]{:S(2)}, u32[]{:S(2)}) collective-permute-start(f32[16,512]{1,0:T(8,128)} %softmax_totals.1.stats_0), channel_id=1, source_target_pairs={{0,64},{1,65},{2,66},{3,67},{4,68},{5,69},{6,70},{7,71},{8,72},{9,... | collective-permute-start | bytes 98312 | tf_op jit(solution)/shard_map/totals/ppermute | solution.py:465
  64.2 6.9 %collective-permute-start.1 = (f32[16,512]{1,0:T(8,128)}, f32[16,512]{1,0:T(8,128)S(1)}, u32[]{:S(2)}, u32[]{:S(2)}) collective-permute-start(f32[16,512]{1,0:T(8,128)} %softmax_totals.1.stats_0), channel_id=1, source_target_pairs={{0,32},{1,33},{2,34},{3,35},{4,36},{5,37},{6,38},{7,39},{8,40},{9,... | collective-permute-start | bytes 98312 | tf_op jit(solution)/shard_map/totals/ppermute | solution.py:465
  71.0 1.2 copy-start.5
  71.0 1.2 copy-start.9
  71.0 1.2 copy-start.10
  71.1 1.2 copy-start.11
  71.1 2.0 %collective-permute-start.4 = (bf16[128,16,128]{2,1,0:T(8,128)(2,1)S(1)}, bf16[128,16,128]{2,1,0:T(8,128)(2,1)S(1)}, u32[]{:S(2)}, u32[]{:S(2)}) collective-permute-start(bf16[128,16,128]{2,1,0:T(8,128)(2,1)S(1)} %slice.10), channel_id=1, source_target_pairs={{0,1},{1,0},{2,3},{3,2},{4,5},{5,4},{6,7},{7,6},{8,9},{9,8},{10,11... | collective-permute-start | bytes 1572872 | tf_op jit(solution)/shard_map/totals/ppermute | solution.py:467
  73.1 0.8 copy-start.8
  103.1 2.9 %collective-permute-start.5 = (bf16[128,32,128]{2,1,0:T(8,128)(2,1)}, bf16[128,32,128]{2,1,0:T(8,128)(2,1)S(1)}, u32[]{:S(2)}, u32[]{:S(2)}) collective-permute-start(bf16[128,32,128]{2,1,0:T(8,128)(2,1)} %get-tuple-element.16), channel_id=1, source_target_pairs={{0,1},{1,0},{2,3},{3,2},{4,5},{5,4},{6,7},{7,6},{8,9},{9,8},{10,11... | collective-permute-start | bytes 3145736 | tf_op jit(solution)/shard_map/exchange_out/ppermute | solution.py:474
  105.9 1.6 %copy-start = (bf16[128,64,128]{2,1,0:T(8,128)(2,1)S(1)}, bf16[128,64,128]{2,1,0:T(8,128)(2,1)}, u32[]{:S(2)}) copy-start(bf16[128,64,128]{2,1,0:T(8,128)(2,1)} %get-tuple-element.15.own) | copy-start | bytes 6291460

commit v3 on v2

v3 whole, which is shorter than its diff:
```python
import jax
import jax.numpy as jnp
from jax import lax
from jax.experimental import pallas as pl
from jax.experimental.pallas import tpu as pltpu
from jax.sharding import PartitionSpec as P

ALL = ("qrow", "kcol")
DEVICES = 128
HEADS = 8
WIDTH = 128
STRETCH = 128
PLACES = 128
KEY_GROUPS = 4
ROW_GROUPS = 32
QUERY_TOKENS = 16
TOKEN_GROUPS = STRETCH // QUERY_TOKENS
PAIR = 2
HEAD_GROUPS = HEADS // PAIR
KEY_TOKENS = STRETCH // KEY_GROUPS
HALF = KEY_TOKENS // 2
ROWS = QUERY_TOKENS * PAIR
ALL_ROWS = PLACES * ROWS
ALL_KEYS = PLACES * KEY_TOKENS
TILE = 512
TILES = ALL_ROWS // TILE
SPAN = TILE // ROWS
SUBLANES = 8
SKEW = 2
PART = 512
PARTS = 2 * TILE // PART
CHUNK = 128
NEGATIVE = -1e30
SCALE = float(WIDTH) ** (-0.5)
TO_LOG2 = SCALE * 1.4426950408889634
MIB = 1024 * 1024


def contract(left, right, left_dim, right_dim):
    return lax.dot_general(
        left, right, (((left_dim,), (right_dim,)), ((), ())), preferred_element_type=jnp.float32
    )


def tile_at(index):
    return pl.ds(pl.multiple_of(index * TILE, TILE), TILE)


def allowed_on_diagonal(key_group, row_group, row_dim):
    row = lax.broadcasted_iota(jnp.int32, (TILE, TILE), row_dim)
    column = lax.broadcasted_iota(jnp.int32, (TILE, TILE), 1 - row_dim)
    first_token = (row_group // HEAD_GROUPS) * QUERY_TOKENS
    row_place = (row // ROWS) * STRETCH + first_token + row % QUERY_TOKENS
    key_place = (column // KEY_TOKENS) * STRETCH + key_group * KEY_TOKENS + column % KEY_TOKENS
    return key_place <= row_place


def stats_kernel(table, scored, other_half, stats, query, key):
    key_group, row_group, core = table[PLACES], table[PLACES + 1], table[PLACES + 2]

    def sort(place, carry):
        source = table[place]
        query[pl.ds(pl.multiple_of(place * ROWS, ROWS), ROWS)] = scored[source, 0:ROWS]
        first = pl.multiple_of(place * KEY_TOKENS + core * HALF, HALF)
        second = pl.multiple_of(place * KEY_TOKENS + (1 - core) * HALF, HALF)
        key[pl.ds(first, HALF)] = scored[source, ROWS : ROWS + HALF]
        key[pl.ds(second, HALF)] = other_half[source, 0:HALF]
        return carry

    lax.fori_loop(0, PLACES, sort, 0, unroll=8)

    def absorb(keys, rows, state, allowed):
        scores = contract(keys, rows, 1, 1)
        if allowed is not None:
            scores = jnp.where(allowed, scores, NEGATIVE)
        highest, summed = state
        scores = scores.reshape(keys.shape[0] // SUBLANES, SUBLANES, rows.shape[0])
        raised = jnp.maximum(highest, jnp.max(scores, axis=0))
        summed = summed * jnp.exp2((highest - raised) * TO_LOG2)
        return raised, summed + jnp.sum(jnp.exp2((scores - raised[None]) * TO_LOG2), axis=0)

    allowed = allowed_on_diagonal(key_group, row_group, 1)
    def per_row_pair(i, carry):
        rows = [
            query[pl.ds(pl.multiple_of(i * 2 * TILE + k * PART, PART), PART)] for k in range(PARTS)
        ]

        def keys_at(j, n):
            return key[pl.ds(pl.multiple_of(j * TILE + n * CHUNK, CHUNK), CHUNK)]

        def full_tile(j, state):
            state = list(state)
            for n in range(TILE // CHUNK):
                keys = keys_at(j, n)
                for k in range(PARTS):
                    state[k] = absorb(keys, rows[k], state[k], None)
            return tuple(state)

        start = (
            jnp.full((SUBLANES, PART), NEGATIVE, jnp.float32),
            jnp.zeros((SUBLANES, PART), jnp.float32),
        )
        state = list(lax.fori_loop(0, 2 * i, full_tile, (start,) * PARTS))
        for n in range(TILE // CHUNK):
            keys = keys_at(2 * i, n)
            for k in range(PARTS):
                mask = None
                if k < PARTS // 2:
                    mask = allowed[n * CHUNK : (n + 1) * CHUNK, k * PART : (k + 1) * PART]
                state[k] = absorb(keys, rows[k], state[k], mask)
            keys = keys_at(2 * i + 1, n)
            for k in range(PARTS // 2):
                mask = allowed[n * CHUNK : (n + 1) * CHUNK, k * PART : (k + 1) * PART]
                late = k + PARTS // 2
                state[late] = absorb(keys, rows[late], state[late], mask)
        for k in range(PARTS):
            highest, summed = state[k]
            row_peak = jnp.max(highest, axis=0, keepdims=True)
            row_total = jnp.sum(
                summed * jnp.exp2((highest - row_peak) * TO_LOG2), axis=0, keepdims=True
            )
            tile = 2 * i + k // (PARTS // 2)
            lanes = (k % (PARTS // 2)) * PART
            stats[pl.ds(tile, 1), lanes : lanes + PART] = row_peak
            stats[pl.ds(tile + TILES, 1), lanes : lanes + PART] = row_total
        return carry

    lax.fori_loop(0, TILES // 2, per_row_pair, 0)


def gradient_kernel(
    table,
    scored,
    other_half,
    weighed,
    stats_0,
    stats_1,
    stats_2,
    stats_3,
    own_grad,
    other_grad,
    query,
    grad,
    query_turned,
    grad_turned,
    key,
    value,
    logs,
    key_sorted,
    value_sorted,
):
    key_group, row_group, core = table[PLACES], table[PLACES + 1], table[PLACES + 2]
    lane = lax.broadcasted_iota(jnp.int32, (TILE, WIDTH), 1)
    row_token = lax.broadcasted_iota(jnp.int32, (ROWS, WIDTH), 0) % QUERY_TOKENS
    row_token = row_token + (row_group // HEAD_GROUPS) * QUERY_TOKENS
    own_lane = lax.broadcasted_iota(jnp.int32, (ROWS, WIDTH), 1) == row_token
    all_stats = [ref[...] for ref in (stats_0, stats_1, stats_2, stats_3)]
    peaks = [part[0:TILES] for part in all_stats]
    highest = jnp.maximum(jnp.maximum(peaks[0], peaks[1]), jnp.maximum(peaks[2], peaks[3]))
    summed = jnp.zeros_like(highest)
    for part in all_stats:
        summed = summed + part[TILES:] * jnp.exp2((part[0:TILES] - highest) * TO_LOG2)
    log_totals = highest + jnp.log2(summed) * (1.0 / TO_LOG2)
    high = log_totals.astype(jnp.bfloat16).astype(jnp.float32)
    middle = (log_totals - high).astype(jnp.bfloat16).astype(jnp.float32)
    low = (log_totals - high - middle).astype(jnp.bfloat16).astype(jnp.float32)
    padding = jnp.zeros((WIDTH - 3 * TILES, TILE), jnp.float32)
    logs[...] = jnp.concatenate([high, middle, low, padding], axis=0).T
    allowed = allowed_on_diagonal(key_group, row_group, 0)
    key_extra = jnp.where(lane < 3 * TILES, -1.0, 0.0).astype(jnp.bfloat16)
    value_extra = jnp.full((TILE, WIDTH), -1.0, jnp.bfloat16)

    def tile_span(t):
        return slice(t * TILE, (t + 1) * TILE)

    def prepare_rows(r):
        here = tile_span(r)
        chosen = jnp.logical_and(lane % TILES == r, lane < 3 * TILES)
        query[here, WIDTH:] = jnp.where(chosen, logs[...], 0.0).astype(jnp.bfloat16)
        for k in range(SPAN):
            source = table[r * SPAN + k]
            spot = slice(r * TILE + k * ROWS, r * TILE + (k + 1) * ROWS)
            query[spot, 0:WIDTH] = scored[source, 0:ROWS]
            grad[spot, 0:WIDTH] = weighed[source, 0:ROWS]
            delta = weighed[source, ROWS : ROWS + SUBLANES].astype(jnp.float32)
            per_row = [
                jnp.broadcast_to(delta[h : h + 1], (QUERY_TOKENS, WIDTH)) for h in range(PAIR)
            ]
            grad[spot, WIDTH:] = jnp.where(own_lane, jnp.concatenate(per_row, axis=0), 0.0).astype(
                jnp.bfloat16
            )
        query_turned[:, here] = query[here, 0:WIDTH].T
        grad_turned[:, here] = grad[here, 0:WIDTH].T

    def prepare_keys(k):
        here = tile_span(k)
        key[here, WIDTH:] = key_extra
        value[here, WIDTH:] = value_extra
        for s in range(SPAN):
            source = table[k * SPAN + s]
            start = k * TILE + s * KEY_TOKENS
            own_spot = pl.ds(pl.multiple_of(start + core * HALF, HALF), HALF)
            other_spot = pl.ds(pl.multiple_of(start + (1 - core) * HALF, HALF), HALF)
            key[own_spot, 0:WIDTH] = scored[source, ROWS : ROWS + HALF]
            key[other_spot, 0:WIDTH] = other_half[source, 0:HALF]
            value[own_spot, 0:WIDTH] = scored[source, ROWS + HALF : ROWS + 2 * HALF]
            value[other_spot, 0:WIDTH] = other_half[source, HALF : 2 * HALF]

    def first(r, k):
        scores = contract(query[tile_span(r)], key[tile_span(k)], 1, 1)
        probs = jnp.exp2(scores * TO_LOG2)
        if r == k:
            probs = jnp.where(allowed, probs, 0.0)
        moved_probs = contract(grad[tile_span(r)], value[tile_span(k)], 1, 1)
        return probs.astype(jnp.bfloat16), (probs * moved_probs).astype(jnp.bfloat16)

    value_sums, key_sums, query_sums = {}, {}, {}

    def add(sums, spot, part):
        sums[spot] = sums[spot] + part if spot in sums else part

    def second(r, k, probs_low, dscores):
        add(value_sums, k, contract(grad_turned[:, tile_span(r)], probs_low, 1, 0))
        add(key_sums, k, contract(query_turned[:, tile_span(r)], dscores, 1, 0))
        add(query_sums, r, contract(dscores, key[tile_span(k), 0:WIDTH], 1, 0))
        if r == k:
            total = (query_sums.pop(r) * SCALE).astype(jnp.bfloat16)
            for s in range(SPAN):
                own_grad[table[r * SPAN + s], 0:ROWS] = total[s * ROWS : (s + 1) * ROWS]
        if r == TILES - 1:
            key_part = (key_sums.pop(k) * SCALE).astype(jnp.bfloat16).T
            value_part = value_sums.pop(k).astype(jnp.bfloat16).T
            key_sorted[tile_span(k)] = key_part
            value_sorted[tile_span(k)] = value_part

    waiting = []
    for k in range(TILES):
        prepare_keys(k)
        for r in range(k, TILES):
            if k == 0:
                prepare_rows(r)
            waiting.append((r, k) + first(r, k))
            if len(waiting) > SKEW:
                second(*waiting.pop(0))
    for entry in waiting:
        second(*entry)

    def unsort(place, carry):
        source = table[place]
        first = pl.ds(pl.multiple_of(place * KEY_TOKENS + core * HALF, HALF), HALF)
        second = pl.ds(pl.multiple_of(place * KEY_TOKENS + (1 - core) * HALF, HALF), HALF)
        own_grad[source, ROWS : ROWS + HALF] = key_sorted[first]
        own_grad[source, ROWS + HALF :] = value_sorted[first]
        other_grad[source, 0:HALF] = key_sorted[second]
        other_grad[source, HALF:] = value_sorted[second]
        return carry

    lax.fori_loop(0, PLACES, unsort, 0, unroll=8)


IN_VMEM = pl.BlockSpec(memory_space=pltpu.VMEM)
IN_SMEM = pl.BlockSpec(memory_space=pltpu.SMEM)
PAIRS = TILE * TILE * TILES * (TILES + 1) // 2


def stats_call(table, scored, other_half):
    return pl.pallas_call(
        stats_kernel,
        out_shape=jax.ShapeDtypeStruct((2 * TILES, TILE), jnp.float32),
        in_specs=[IN_SMEM, IN_VMEM, IN_VMEM],
        out_specs=IN_VMEM,
        scratch_shapes=[
            pltpu.VMEM((ALL_ROWS, WIDTH), jnp.bfloat16),
            pltpu.VMEM((ALL_KEYS, WIDTH), jnp.bfloat16),
        ],
        compiler_params=pltpu.CompilerParams(vmem_limit_bytes=20 * MIB),
        cost_estimate=pl.CostEstimate(
            flops=2 * PAIRS * WIDTH, bytes_accessed=4 * MIB, transcendentals=PAIRS
        ),
        name="softmax_totals",
    )(table, scored, other_half)


def gradient_call(table, scored, other_half, weighed, stats):
    own = jax.ShapeDtypeStruct((PLACES, ROWS + 2 * HALF, WIDTH), jnp.bfloat16)
    other = jax.ShapeDtypeStruct((PLACES, 2 * HALF, WIDTH), jnp.bfloat16)
    return pl.pallas_call(
        gradient_kernel,
        out_shape=(own, other),
        in_specs=[IN_SMEM] + [IN_VMEM] * 7,
        out_specs=(IN_VMEM,) * 2,
        scratch_shapes=[
            pltpu.VMEM((ALL_ROWS, 2 * WIDTH), jnp.bfloat16),
            pltpu.VMEM((ALL_ROWS, 2 * WIDTH), jnp.bfloat16),
            pltpu.VMEM((WIDTH, ALL_ROWS), jnp.bfloat16),
            pltpu.VMEM((WIDTH, ALL_ROWS), jnp.bfloat16),
            pltpu.VMEM((ALL_KEYS, 2 * WIDTH), jnp.bfloat16),
            pltpu.VMEM((ALL_KEYS, 2 * WIDTH), jnp.bfloat16),
            pltpu.VMEM((TILE, WIDTH), jnp.float32),
            pltpu.VMEM((ALL_KEYS, WIDTH), jnp.bfloat16),
            pltpu.VMEM((ALL_KEYS, WIDTH), jnp.bfloat16),
        ],
        compiler_params=pltpu.CompilerParams(vmem_limit_bytes=32 * MIB),
        cost_estimate=pl.CostEstimate(
            flops=10 * PAIRS * WIDTH, bytes_accessed=8 * MIB, transcendentals=PAIRS
        ),
        name="gradients",
    )(table, scored, other_half, weighed, *stats)


def pack_rows(rows, outgoing):
    for r in range(ROW_GROUPS):
        tokens = (r // HEAD_GROUPS) * QUERY_TOKENS
        for h in range(PAIR):
            head = (r % HEAD_GROUPS) * PAIR + h
            part = rows[tokens : tokens + QUERY_TOKENS, head * WIDTH : (head + 1) * WIDTH]
            for g in range(KEY_GROUPS):
                outgoing[
                    g * ROW_GROUPS + r, h * QUERY_TOKENS : (h + 1) * QUERY_TOKENS
                ] = part


def pack_kernel(rows, keys, values, outgoing):
    pack_rows(rows, outgoing)
    for g in range(KEY_GROUPS):
        for c in range(2):
            first = g * KEY_TOKENS + c * HALF
            for n, array in enumerate((keys, values)):
                part = array[first : first + HALF]
                spot = slice(ROWS + n * HALF, ROWS + (n + 1) * HALF)
                for r in range(c, ROW_GROUPS, 2):
                    outgoing[g * ROW_GROUPS + r, spot] = part


def pack_grad_kernel(rows, forward, outgoing):
    pack_rows(rows, outgoing)
    lane = lax.broadcasted_iota(jnp.int32, (STRETCH, WIDTH), 1)
    delta = jnp.zeros((STRETCH, WIDTH), jnp.float32)
    for head in range(HEADS):
        span = slice(head * WIDTH, (head + 1) * WIDTH)
        products = rows[:, span].astype(jnp.float32) * forward[:, span].astype(jnp.float32)
        delta = jnp.where(lane == head, jnp.sum(products, axis=1, keepdims=True), delta)
    delta = delta.T
    blank = jnp.zeros((SUBLANES - PAIR, WIDTH), jnp.float32)
    for p in range(HEAD_GROUPS):
        part = jnp.concatenate([delta[PAIR * p : PAIR * (p + 1)], blank], axis=0)
        part = part.astype(jnp.bfloat16)
        for r in range(p, DEVICES, HEAD_GROUPS):
            outgoing[r, ROWS : ROWS + SUBLANES] = part


def pack_call(kernel, height, *arrays):
    return pl.pallas_call(
        kernel,
        out_shape=jax.ShapeDtypeStruct((DEVICES, height, WIDTH), jnp.bfloat16),
        in_specs=[IN_VMEM] * len(arrays),
        out_specs=IN_VMEM,
        compiler_params=pltpu.CompilerParams(vmem_limit_bytes=56 * MIB),
        name="pack",
    )(*arrays)


def pair_kernel(own, received, outgoing):
    outgoing[:, 0:ROWS] = own[:, 0:ROWS]
    total = own[:, ROWS:].astype(jnp.float32) + received[...].astype(jnp.float32)
    outgoing[:, ROWS:] = total.astype(jnp.bfloat16)


def pair_call(own, received):
    return pl.pallas_call(
        pair_kernel,
        out_shape=jax.ShapeDtypeStruct(own.shape, own.dtype),
        in_specs=[IN_VMEM] * 2,
        out_specs=IN_VMEM,
        compiler_params=pltpu.CompilerParams(vmem_limit_bytes=16 * MIB),
        name="pair_sum",
    )(own, received)


def sums_kernel(back, d_query, d_key, d_value):
    for r in range(ROW_GROUPS):
        total = back[r, 0:ROWS].astype(jnp.float32)
        for g in range(1, KEY_GROUPS):
            total = total + back[g * ROW_GROUPS + r, 0:ROWS].astype(jnp.float32)
        total = total.astype(jnp.bfloat16)
        tokens = (r // HEAD_GROUPS) * QUERY_TOKENS
        for h in range(PAIR):
            head = (r % HEAD_GROUPS) * PAIR + h
            d_query[tokens : tokens + QUERY_TOKENS, head * WIDTH : (head + 1) * WIDTH] = total[
                h * QUERY_TOKENS : (h + 1) * QUERY_TOKENS
            ]
    for g in range(KEY_GROUPS):
        for c in range(2):
            total = jnp.zeros((2 * HALF, WIDTH), jnp.float32)
            for r in range(c, ROW_GROUPS, 2):
                total = total + back[g * ROW_GROUPS + r, ROWS:].astype(jnp.float32)
            first = g * KEY_TOKENS + c * HALF
            d_key[first : first + HALF] = total[0:HALF].astype(jnp.bfloat16)
            d_value[first : first + HALF] = total[HALF:].astype(jnp.bfloat16)


def sums_call(back):
    small = jax.ShapeDtypeStruct((STRETCH, WIDTH), jnp.bfloat16)
    return pl.pallas_call(
        sums_kernel,
        out_shape=(
            jax.ShapeDtypeStruct((STRETCH, HEADS * WIDTH), jnp.bfloat16),
            small,
            small,
        ),
        in_specs=[IN_VMEM],
        out_specs=(IN_VMEM,) * 3,
        compiler_params=pltpu.CompilerParams(vmem_limit_bytes=12 * MIB),
        name="sums",
    )(back)


def shards(queries, key_states, value_states, out_grad, forward_out, stretch_order):
    me = lax.axis_index(ALL)
    swap = [(d, d ^ 1) for d in range(DEVICES)]

    def around(step):
        return [(d, (d + step * ROW_GROUPS) % DEVICES) for d in range(DEVICES)]

    with jax.named_scope("outgoing"):
        scored = pack_call(pack_kernel, ROWS + 2 * HALF, queries, key_states, value_states)
        weighed = pack_call(pack_grad_kernel, ROWS + SUBLANES, out_grad, forward_out)
    with jax.named_scope("table"):
        places = jnp.arange(PLACES, dtype=jnp.int32)
        holder = jnp.sum(
            jnp.where(stretch_order[None, :] == places[:, None], places[None, :], 0), axis=1
        )
        ids = jnp.stack([me // ROW_GROUPS, me % ROW_GROUPS, me % 2]).astype(jnp.int32)
        table = jnp.concatenate([holder, ids])
    with jax.named_scope("exchange_in"):
        scored = lax.all_to_all(scored, ALL, split_axis=0, concat_axis=0, tiled=True)
        scored, weighed = lax.optimization_barrier((scored, weighed))
        weighed = lax.all_to_all(weighed, ALL, split_axis=0, concat_axis=0, tiled=True)
        other_half = lax.ppermute(scored[:, ROWS:], ALL, swap)
    with jax.named_scope("totals"):
        stats = stats_call(table, scored, other_half)
        all_stats = [stats] + [lax.ppermute(stats, ALL, around(k)) for k in range(1, KEY_GROUPS)]
        weighed, all_stats = lax.optimization_barrier((weighed, all_stats))
    with jax.named_scope("gradients"):
        own_grad, other_grad = gradient_call(
            table, scored, other_half, weighed, all_stats
        )
    with jax.named_scope("exchange_out"):
        received = lax.ppermute(other_grad, ALL, swap)
        outgoing = pair_call(own_grad, received)
        back = lax.all_to_all(outgoing, ALL, split_axis=0, concat_axis=0, tiled=True)
    with jax.named_scope("sums"):
        return sums_call(back)


def solution(mesh):
    split = P(ALL, None)
    return jax.shard_map(
        shards,
        mesh=mesh,
        in_specs=(split,) * 5 + (P(),),
        out_specs=(split,) * 3,
        check_vma=False,
    )
```

time: 146 us -> 139 us (0.952)
  local copies, waits for them, and re-layouts: 6.52 us -> 1.13 us
  other arithmetic: 3.18 us -> 0.18 us
  Pallas kernels: 46.2 us -> 44.2 us
  waiting for transfers between devices: 32.3 us -> 34.2 us
    all_to_all x1, waiting for transfers between devices: 5.97 us -> 0.01 us  [shards(): lax.all_to_all(weighed, ALL, split_axis=0, concat_axis=0, tiled=True)]
    all_to_all x1, waiting for transfers between devices: 21.9 us -> 27.3 us  [shards(): lax.all_to_all(scored, ALL, split_axis=0, concat_axis=0, tiled=True)]
    unnamed x27 -> x2, local copies, waits for them, and re-layouts: 4.87 us -> 0.01 us
    pallas_call x1, Pallas kernels: 29.2 us -> 24.5 us  [gradient_call(): pl.pallas_call(gradient_kernel, out_shape=(own, other), in_specs=[IN_SMEM...]
    ppermute x3, waiting for transfers between devices: 0.01 us -> 4.27 us  [shards(): lax.ppermute(stats, ALL, around(k))]
    pallas_call x2, Pallas kernels: 1.56 us -> 5.08 us  [pack_call(): pl.pallas_call(kernel, out_shape=jax.ShapeDtypeStruct((DEVICES, height, W...]
    ppermute x2 -> x1, waiting for transfers between devices: 1.65 us -> 0.01 us  [shards(): other_half = lax.ppermute(scored[:, ROWS:], ALL, swap)]
    concatenate x1 -> x0, other arithmetic: 1.47 us -> none  [shards(): jnp.concatenate([pack_call(out_grad, value_states), jnp.tile(delta, (KEY_...]
  transfers between devices with their start and end apart: 8 -> 7, of which waited for: 5 -> 5; matrix products, arithmetic and copies ran while one was open for 3% -> 0% of each run, Pallas kernels for 10% -> 11%
where the time goes in v3:
time: 139 us
  Pallas kernels  44.2 us (32%)
  blocking collectives  38.3 us (28%)
  waiting for transfers between devices  34.2 us (25%)
  starting transfers between devices  19.9 us (14%)
    all_to_all x1, blocking collectives, shards(): lax.all_to_all(outgoing, ALL, split_axis=0, concat_axis=0, tiled=True)  38.3 us
    all_to_all x1, waiting for transfers between devices, shards(): lax.all_to_all(scored, ALL, split_axis=0, concat_axis=0, tiled=True)  27.3 us
    pallas_call x1, Pallas kernels, gradient_call(): pl.pallas_call(gradient_kernel, out_shape=(own, other), in_specs=[IN_SMEM...  24.5 us
    pallas_call x1, Pallas kernels, stats_call(): pl.pallas_call(stats_kernel, out_shape=jax.ShapeDtypeStruct((2 * TILES, T...  13.4 us
    all_to_all x1, starting transfers between devices, shards(): lax.all_to_all(scored, ALL, split_axis=0, concat_axis=0, tiled=True)  11.1 us
    pallas_call x2, Pallas kernels, pack_call(): pl.pallas_call(kernel, out_shape=jax.ShapeDtypeStruct((DEVICES, height, W...  5.08 us
    all_to_all x1, starting transfers between devices, shards(): lax.all_to_all(weighed, ALL, split_axis=0, concat_axis=0, tiled=True)  4.77 us
    ppermute x3, waiting for transfers between devices, shards(): lax.ppermute(stats, ALL, around(k))  4.27 us
  transfers between devices with their start and end apart: 7, of which 5 were waited for; matrix products, arithmetic and copies ran while one was open for 0% of the time, Pallas kernels for 11%

profile of v3, /device:TPU:0, one launch (start us, length us, event | category | flops | bytes accessed | tf_op | source)
XLA Modules:
  0.0 138.7 jit_solution(8000412912586760415)
XLA Ops:
  0.6 2.7 %pack.2 = bf16[128,64,128]{2,1,0:T(8,128)(2,1)} custom-call(bf16[128,1024]{1,0:T(8,128)(2,1)} %rows.2, bf16[128,128]{1,0:T(8,128)(2,1)} %keys.1, bf16[128,128]{1,0:T(8,128)(2,1)} %values.1), custom_call_target="tpu_custom_call" | custom-call | tf_op jit(solution)/shard_map/outgoing/pack/pallas_call | solution.py:353
  3.3 11.1 %all-to-all-start = ((bf16[128,64,128]{2,1,0:T(8,128)(2,1)}), bf16[128,64,128]{2,1,0:T(8,128)(2,1)S(1)}, u32[]{:S(2)}, u32[]{:S(2)}) async-start(bf16[128,64,128]{2,1,0:T(8,128)(2,1)} %pack.2), calls=%async_computation | async-start | bytes 4194304 | tf_op jit(solution)/shard_map/exchange_in/all_to_all | solution.py:436
  14.4 2.4 %pack.3 = bf16[128,40,128]{2,1,0:T(8,128)(2,1)} custom-call(bf16[128,1024]{1,0:T(8,128)(2,1)} %rows.3, bf16[128,1024]{1,0:T(8,128)(2,1)} %forward.1), custom_call_target="tpu_custom_call" | custom-call | tf_op jit(solution)/shard_map/outgoing/pack/pallas_call | solution.py:353
  16.9 0.0 copy-start
  16.9 27.3 %all-to-all-done.scored = bf16[128,64,128]{2,1,0:T(8,128)(2,1)S(1)} async-done(((bf16[128,64,128]{2,1,0:T(8,128)(2,1)}), bf16[128,64,128]{2,1,0:T(8,128)(2,1)S(1)}, u32[]{:S(2)}, u32[]{:S(2)}) %all-to-all-start) | async-done | bytes 2097184 | tf_op jit(solution)/shard_map/exchange_in/all_to_all | solution.py:436
  44.1 1.1 slice.3
  45.3 0.0 collective-permute-start
  45.3 4.8 %all-to-all-start.1 = ((bf16[128,40,128]{2,1,0:T(8,128)(2,1)}), bf16[128,40,128]{2,1,0:T(8,128)(2,1)S(1)}, u32[]{:S(2)}, u32[]{:S(2)}) async-start(bf16[128,40,128]{2,1,0:T(8,128)(2,1)} %pack.3), calls=%async_computation.1 | async-start | bytes 2621440 | tf_op jit(solution)/shard_map/exchange_in/all_to_all | solution.py:438
  50.1 0.0 copy-done
  50.1 0.1 select_reduce_fusion
  50.2 0.1 pad_add_fusion.table
  50.3 0.0 collective-permute-done.other_half
  50.3 13.4 %softmax_totals.1.stats_0 = f32[16,512]{1,0:T(8,128)S(1)} custom-call(s32[131]{0:T(256)S(1)} %pad_add_fusion.table, bf16[128,64,128]{2,1,0:T(8,128)(2,1)S(1)} %all-to-all-done.scored, bf16[128,32,128]{2,1,0:T(8,128)(2,1)} %collective-permute-done.other_half), custom_call_target="tpu_custom_call" | custom-call | flops 2415919104 | bytes 4194304 | tf_op jit(solution)/shard_map/totals/softmax_totals/pallas_call | solution.py:267
  63.7 2.2 %collective-permute-start.3 = (f32[16,512]{1,0:T(8,128)S(1)}, f32[16,512]{1,0:T(8,128)S(1)}, u32[]{:S(2)}, u32[]{:S(2)}) collective-permute-start(f32[16,512]{1,0:T(8,128)S(1)} %softmax_totals.1.stats_0), channel_id=1, source_target_pairs={{0,96},{1,97},{2,98},{3,99},{4,100},{5,101},{6,102},{7,103},{8,104... | collective-permute-start | bytes 98312 | tf_op jit(solution)/shard_map/totals/ppermute | solution.py:442
  65.9 0.9 collective-permute-start.2
  66.8 0.9 collective-permute-start.1
  67.6 0.1 collective-permute-done.3.stats_3
  67.7 3.6 %collective-permute-done.2.stats_2 = f32[16,512]{1,0:T(8,128)S(1)} collective-permute-done((f32[16,512]{1,0:T(8,128)S(1)}, f32[16,512]{1,0:T(8,128)S(1)}, u32[]{:S(2)}, u32[]{:S(2)}) %collective-permute-start.2) | collective-permute-done | bytes 32800 | tf_op jit(solution)/shard_map/totals/ppermute | solution.py:442
  71.3 0.6 collective-permute-done.1.stats_1
  71.9 0.0 all-to-all-done.1.weighed
  71.9 24.5 %gradients.1 = (bf16[128,64,128]{2,1,0:T(8,128)(2,1)S(1)}, bf16[128,32,128]{2,1,0:T(8,128)(2,1)S(1)}) custom-call(s32[131]{0:T(256)S(1)} %pad_add_fusion.table, bf16[128,64,128]{2,1,0:T(8,128)(2,1)S(1)} %all-to-all-done.scored, bf16[128,32,128]{2,1,0:T(8,128)(2,1)} %collective-permute-done.other_half, bf16[128,40,128]{2,1,0:T(8,128)(2,1)S(1)} %all-to-all-done.1.weighed, ...), custom_call_target="tpu_custom_call" | custom-call | flops 12079595520 | bytes 8388608 | tf_op jit(solution)/shard_map/gradients/gradients/pallas_call | solution.py:287
  96.4 0.1 collective-permute-start.4
  96.5 2.6 %collective-permute-done.4.received = bf16[128,32,128]{2,1,0:T(8,128)(2,1)S(1)} collective-permute-done((bf16[128,32,128]{2,1,0:T(8,128)(2,1)S(1)}, bf16[128,32,128]{2,1,0:T(8,128)(2,1)S(1)}, u32[]{:S(2)}, u32[]{:S(2)}) %collective-permute-start.4) | collective-permute-done | bytes 1048608 | tf_op jit(solution)/shard_map/exchange_out/ppermute | solution.py:449
  99.2 0.3 pair_sum.1
  99.5 38.3 %all_to_all.15.back = bf16[128,64,128]{2,1,0:T(8,128)(2,1)S(1)} all-to-all(bf16[128,64,128]{2,1,0:T(8,128)(2,1)S(1)} %pair_sum.1), channel_id=1, replica_groups=mesh['qrow'=32,'kcol'=4] {'qrow','kcol'}, dimensions={0} | all-to-all | bytes 4194304 | tf_op jit(solution)/shard_map/exchange_out/all_to_all | solution.py:451
  137.8 0.9 sums.1
Async XLA Ops:
  3.3 40.9 %all-to-all-start = ((bf16[128,64,128]{2,1,0:T(8,128)(2,1)}), bf16[128,64,128]{2,1,0:T(8,128)(2,1)S(1)}, u32[]{:S(2)}, u32[]{:S(2)}) async-start(bf16[128,64,128]{2,1,0:T(8,128)(2,1)} %pack.2), calls=%async_computation | async-start | bytes 4194304 | tf_op jit(solution)/shard_map/exchange_in/all_to_all | solution.py:436
  16.9 33.2 %copy-start = (s32[128]{0:T(128)S(1)}, s32[128]{0:T(128)}, u32[]{:S(2)}) copy-start(s32[128]{0:T(128)} %param.11) | copy-start | bytes 1540
  45.3 5.0 %collective-permute-start = (bf16[128,32,128]{2,1,0:T(8,128)(2,1)}, bf16[128,32,128]{2,1,0:T(8,128)(2,1)}, u32[]{:S(2)}, u32[]{:S(2)}) collective-permute-start(bf16[128,32,128]{2,1,0:T(8,128)(2,1)} %slice.3), channel_id=1, source_target_pairs={{0,1},{1,0},{2,3},{3,2},{4,5},{5,4},{6,7},{7,6},{8,9},{9,8},{10,11... | collective-permute-start | bytes 3145736 | tf_op jit(solution)/shard_map/exchange_in/ppermute | solution.py:439
  45.3 26.6 %all-to-all-start.1 = ((bf16[128,40,128]{2,1,0:T(8,128)(2,1)}), bf16[128,40,128]{2,1,0:T(8,128)(2,1)S(1)}, u32[]{:S(2)}, u32[]{:S(2)}) async-start(bf16[128,40,128]{2,1,0:T(8,128)(2,1)} %pack.3), calls=%async_computation.1 | async-start | bytes 2621440 | tf_op jit(solution)/shard_map/exchange_in/all_to_all | solution.py:438
  63.7 4.0 %collective-permute-start.3 = (f32[16,512]{1,0:T(8,128)S(1)}, f32[16,512]{1,0:T(8,128)S(1)}, u32[]{:S(2)}, u32[]{:S(2)}) collective-permute-start(f32[16,512]{1,0:T(8,128)S(1)} %softmax_totals.1.stats_0), channel_id=1, source_target_pairs={{0,96},{1,97},{2,98},{3,99},{4,100},{5,101},{6,102},{7,103},{8,104... | collective-permute-start | bytes 98312 | tf_op jit(solution)/shard_map/totals/ppermute | solution.py:442
  65.9 5.4 %collective-permute-start.2 = (f32[16,512]{1,0:T(8,128)S(1)}, f32[16,512]{1,0:T(8,128)S(1)}, u32[]{:S(2)}, u32[]{:S(2)}) collective-permute-start(f32[16,512]{1,0:T(8,128)S(1)} %softmax_totals.1.stats_0), channel_id=1, source_target_pairs={{0,64},{1,65},{2,66},{3,67},{4,68},{5,69},{6,70},{7,71},{8,72},{9,... | collective-permute-start | bytes 98312 | tf_op jit(solution)/shard_map/totals/ppermute | solution.py:442
  66.8 5.1 %collective-permute-start.1 = (f32[16,512]{1,0:T(8,128)S(1)}, f32[16,512]{1,0:T(8,128)S(1)}, u32[]{:S(2)}, u32[]{:S(2)}) collective-permute-start(f32[16,512]{1,0:T(8,128)S(1)} %softmax_totals.1.stats_0), channel_id=1, source_target_pairs={{0,32},{1,33},{2,34},{3,35},{4,36},{5,37},{6,38},{7,39},{8,40},{9,... | collective-permute-start | bytes 98312 | tf_op jit(solution)/shard_map/totals/ppermute | solution.py:442
  96.4 2.7 %collective-permute-start.4 = (bf16[128,32,128]{2,1,0:T(8,128)(2,1)S(1)}, bf16[128,32,128]{2,1,0:T(8,128)(2,1)S(1)}, u32[]{:S(2)}, u32[]{:S(2)}) collective-permute-start(bf16[128,32,128]{2,1,0:T(8,128)(2,1)S(1)} %get-tuple-element.20), channel_id=1, source_target_pairs={{0,1},{1,0},{2,3},{3,2},{4,5},{5,4},{6,7},{7,6},{8,9},{9,8},{10,11... | collective-permute-start | bytes 3145736 | tf_op jit(solution)/shard_map/exchange_out/ppermute | solution.py:449

commit v4 on v3

--- a/solution.py
+++ b/solution.py
@@ -26,10 +26,9 @@
 TILES = ALL_ROWS // TILE
 SPAN = TILE // ROWS
 SUBLANES = 8
-SKEW = 2
-PART = 512
-PARTS = 2 * TILE // PART
-CHUNK = 128
+SKEW = 3
+HALF_TILE = TILE // 2
+CHUNK = 256
 NEGATIVE = -1e30
 SCALE = float(WIDTH) ** (-0.5)
 TO_LOG2 = SCALE * 1.4426950408889634
@@ -58,74 +57,62 @@
 def stats_kernel(table, scored, other_half, stats, query, key):
     key_group, row_group, core = table[PLACES], table[PLACES + 1], table[PLACES + 2]
 
-    def sort(place, carry):
-        source = table[place]
-        query[pl.ds(pl.multiple_of(place * ROWS, ROWS), ROWS)] = scored[source, 0:ROWS]
-        first = pl.multiple_of(place * KEY_TOKENS + core * HALF, HALF)
-        second = pl.multiple_of(place * KEY_TOKENS + (1 - core) * HALF, HALF)
-        key[pl.ds(first, HALF)] = scored[source, ROWS : ROWS + HALF]
-        key[pl.ds(second, HALF)] = other_half[source, 0:HALF]
-        return carry
-
-    lax.fori_loop(0, PLACES, sort, 0, unroll=8)
-
-    def absorb(keys, rows, state, allowed):
-        scores = contract(keys, rows, 1, 1)
-        if allowed is not None:
-            scores = jnp.where(allowed, scores, NEGATIVE)
-        highest, summed = state
-        scores = scores.reshape(keys.shape[0] // SUBLANES, SUBLANES, rows.shape[0])
-        raised = jnp.maximum(highest, jnp.max(scores, axis=0))
-        summed = summed * jnp.exp2((highest - raised) * TO_LOG2)
-        return raised, summed + jnp.sum(jnp.exp2((scores - raised[None]) * TO_LOG2), axis=0)
+    def prepare_rows(r):
+        for s in range(SPAN):
+            spot = slice(r * TILE + s * ROWS, r * TILE + (s + 1) * ROWS)
+            scaled = scored[table[r * SPAN + s], 0:ROWS].astype(jnp.float32) * TO_LOG2
+            high = scaled.astype(jnp.bfloat16)
+            query[spot, 0:WIDTH] = high
+            query[spot, WIDTH:] = (scaled - high.astype(jnp.float32)).astype(jnp.bfloat16)
+
+    def prepare_keys(k):
+        for s in range(SPAN):
+            source = table[k * SPAN + s]
+            start = k * TILE + s * KEY_TOKENS
+            own_spot = pl.ds(pl.multiple_of(start + core * HALF, HALF), HALF)
+            other_spot = pl.ds(pl.multiple_of(start + (1 - core) * HALF, HALF), HALF)
+            own = scored[source, ROWS : ROWS + HALF]
+            other = other_half[source, 0:HALF]
+            key[own_spot, 0:WIDTH] = own
+            key[own_spot, WIDTH:] = own
+            key[other_spot, 0:WIDTH] = other
+            key[other_spot, WIDTH:] = other
 
     allowed = allowed_on_diagonal(key_group, row_group, 1)
-    def per_row_pair(i, carry):
-        rows = [
-            query[pl.ds(pl.multiple_of(i * 2 * TILE + k * PART, PART), PART)] for k in range(PARTS)
-        ]
-
-        def keys_at(j, n):
-            return key[pl.ds(pl.multiple_of(j * TILE + n * CHUNK, CHUNK), CHUNK)]
-
-        def full_tile(j, state):
-            state = list(state)
-            for n in range(TILE // CHUNK):
-                keys = keys_at(j, n)
-                for k in range(PARTS):
-                    state[k] = absorb(keys, rows[k], state[k], None)
-            return tuple(state)
-
-        start = (
-            jnp.full((SUBLANES, PART), NEGATIVE, jnp.float32),
-            jnp.zeros((SUBLANES, PART), jnp.float32),
-        )
-        state = list(lax.fori_loop(0, 2 * i, full_tile, (start,) * PARTS))
-        for n in range(TILE // CHUNK):
-            keys = keys_at(2 * i, n)
-            for k in range(PARTS):
-                mask = None
-                if k < PARTS // 2:
-                    mask = allowed[n * CHUNK : (n + 1) * CHUNK, k * PART : (k + 1) * PART]
-                state[k] = absorb(keys, rows[k], state[k], mask)
-            keys = keys_at(2 * i + 1, n)
-            for k in range(PARTS // 2):
-                mask = allowed[n * CHUNK : (n + 1) * CHUNK, k * PART : (k + 1) * PART]
-                late = k + PARTS // 2
-                state[late] = absorb(keys, rows[late], state[late], mask)
-        for k in range(PARTS):
-            highest, summed = state[k]
-            row_peak = jnp.max(highest, axis=0, keepdims=True)
-            row_total = jnp.sum(
-                summed * jnp.exp2((highest - row_peak) * TO_LOG2), axis=0, keepdims=True
-            )
-            tile = 2 * i + k // (PARTS // 2)
-            lanes = (k % (PARTS // 2)) * PART
-            stats[pl.ds(tile, 1), lanes : lanes + PART] = row_peak
-            stats[pl.ds(tile + TILES, 1), lanes : lanes + PART] = row_total
-        return carry
-
-    lax.fori_loop(0, TILES // 2, per_row_pair, 0)
+    state = {}
+
+    def absorb(r, first, masked):
+        scores = contract(key[first : first + CHUNK], query[r * TILE : (r + 1) * TILE], 1, 1)
+        if masked:
+            inside = first - r * TILE
+            scores = jnp.where(allowed[inside : inside + CHUNK], scores, NEGATIVE)
+        scores = scores.reshape(CHUNK // SUBLANES, SUBLANES, TILE)
+        chunk_peak = jnp.max(scores, axis=0)
+        if r not in state:
+            raised = chunk_peak
+            state[r] = raised, jnp.sum(jnp.exp2(scores - raised[None]), axis=0)
+            return
+        highest, summed = state[r]
+        raised = jnp.maximum(highest, chunk_peak)
+        summed = summed * jnp.exp2(highest - raised)
+        state[r] = raised, summed + jnp.sum(jnp.exp2(scores - raised[None]), axis=0)
+
+    def finish(r):
+        highest, summed = state.pop(r)
+        row_peak = jnp.max(highest, axis=0, keepdims=True)
+        row_total = jnp.sum(summed * jnp.exp2(highest - row_peak), axis=0, keepdims=True)
+        stats[r : r + 1] = row_peak
+        stats[r + TILES : r + TILES + 1] = row_total
+
+    for first in range(0, ALL_KEYS, CHUNK):
+        if first % TILE == 0:
+            prepare_keys(first // TILE)
+        for r in range(first // TILE, TILES):
+            if first == 0:
+                prepare_rows(r)
+            absorb(r, first, r == first // TILE)
+        if (first + CHUNK) % TILE == 0:
+            finish(first // TILE)
 
 
 def gradient_kernel(
@@ -159,8 +146,8 @@
     highest = jnp.maximum(jnp.maximum(peaks[0], peaks[1]), jnp.maximum(peaks[2], peaks[3]))
     summed = jnp.zeros_like(highest)
     for part in all_stats:
-        summed = summed + part[TILES:] * jnp.exp2((part[0:TILES] - highest) * TO_LOG2)
-    log_totals = highest + jnp.log2(summed) * (1.0 / TO_LOG2)
+        summed = summed + part[TILES:] * jnp.exp2(part[0:TILES] - highest)
+    log_totals = (highest + jnp.log2(summed)) * (1.0 / TO_LOG2)
     high = log_totals.astype(jnp.bfloat16).astype(jnp.float32)
     middle = (log_totals - high).astype(jnp.bfloat16).astype(jnp.float32)
     low = (log_totals - high - middle).astype(jnp.bfloat16).astype(jnp.float32)
@@ -206,12 +193,12 @@
             value[own_spot, 0:WIDTH] = scored[source, ROWS + HALF : ROWS + 2 * HALF]
             value[other_spot, 0:WIDTH] = other_half[source, HALF : 2 * HALF]
 
-    def first(r, k):
-        scores = contract(query[tile_span(r)], key[tile_span(k)], 1, 1)
+    def first(rows_at, keys_at, masked):
+        scores = contract(query[rows_at], key[keys_at], 1, 1)
         probs = jnp.exp2(scores * TO_LOG2)
-        if r == k:
-            probs = jnp.where(allowed, probs, 0.0)
-        moved_probs = contract(grad[tile_span(r)], value[tile_span(k)], 1, 1)
+        if masked:
+            probs = jnp.where(allowed[: scores.shape[0], : scores.shape[1]], probs, 0.0)
+        moved_probs = contract(grad[rows_at], value[keys_at], 1, 1)
         return probs.astype(jnp.bfloat16), (probs * moved_probs).astype(jnp.bfloat16)
 
     value_sums, key_sums, query_sums = {}, {}, {}
@@ -219,31 +206,70 @@
     def add(sums, spot, part):
         sums[spot] = sums[spot] + part if spot in sums else part
 
-    def second(r, k, probs_low, dscores):
-        add(value_sums, k, contract(grad_turned[:, tile_span(r)], probs_low, 1, 0))
-        add(key_sums, k, contract(query_turned[:, tile_span(r)], dscores, 1, 0))
-        add(query_sums, r, contract(dscores, key[tile_span(k), 0:WIDTH], 1, 0))
-        if r == k:
-            total = (query_sums.pop(r) * SCALE).astype(jnp.bfloat16)
-            for s in range(SPAN):
-                own_grad[table[r * SPAN + s], 0:ROWS] = total[s * ROWS : (s + 1) * ROWS]
-        if r == TILES - 1:
-            key_part = (key_sums.pop(k) * SCALE).astype(jnp.bfloat16).T
-            value_part = value_sums.pop(k).astype(jnp.bfloat16).T
-            key_sorted[tile_span(k)] = key_part
-            value_sorted[tile_span(k)] = value_part
+    def second(r, k, rows_at, keys_at, probs_low, dscores):
+        value_part = contract(grad_turned[:, rows_at], probs_low, 1, 0)
+        key_part = contract(query_turned[:, rows_at], dscores, 1, 0)
+        query_part = contract(dscores, key[keys_at, 0:WIDTH], 1, 0)
+        row_start = rows_at.start - r * TILE
+        key_start = keys_at.start - k * TILE
+        for n in range((rows_at.stop - rows_at.start) // HALF_TILE):
+            span = slice(n * HALF_TILE, (n + 1) * HALF_TILE)
+            add(query_sums, (r, row_start // HALF_TILE + n), query_part[span])
+        for n in range((keys_at.stop - keys_at.start) // HALF_TILE):
+            span = slice(n * HALF_TILE, (n + 1) * HALF_TILE)
+            add(value_sums, (k, key_start // HALF_TILE + n), value_part[:, span])
+            add(key_sums, (k, key_start // HALF_TILE + n), key_part[:, span])
+
+    def finish_rows(r):
+        for n in range(2):
+            total = (query_sums.pop((r, n)) * SCALE).astype(jnp.bfloat16)
+            for s in range(SPAN // 2):
+                source = table[r * SPAN + n * SPAN // 2 + s]
+                own_grad[source, 0:ROWS] = total[s * ROWS : (s + 1) * ROWS]
+
+    def finish_keys(k):
+        for n in range(2):
+            here = slice(k * TILE + n * HALF_TILE, k * TILE + (n + 1) * HALF_TILE)
+            key_sorted[here] = (key_sums.pop((k, n)) * SCALE).astype(jnp.bfloat16).T
+            value_sorted[here] = value_sums.pop((k, n)).astype(jnp.bfloat16).T
+
+    def blocks():
+        for k in range(TILES):
+            middle = k * TILE + HALF_TILE
+            late = slice(middle, (k + 1) * TILE)
+            yield k, k, tile_span(k), slice(k * TILE, middle), True
+            yield k, k, late, late, True
+            for r in range(k + 1, TILES):
+                yield r, k, tile_span(r), tile_span(k), False
+
+    left = {}
+    for r, k, *_ in blocks():
+        left["rows", r] = left.get(("rows", r), 0) + 1
+        left["keys", k] = left.get(("keys", k), 0) + 1
+
+    def retire(r, k, *rest):
+        second(r, k, *rest)
+        left["rows", r] -= 1
+        left["keys", k] -= 1
+        if left["rows", r] == 0:
+            finish_rows(r)
+        if left["keys", k] == 0:
+            finish_keys(k)
 
     waiting = []
-    for k in range(TILES):
-        prepare_keys(k)
-        for r in range(k, TILES):
-            if k == 0:
-                prepare_rows(r)
-            waiting.append((r, k) + first(r, k))
-            if len(waiting) > SKEW:
-                second(*waiting.pop(0))
+    ready = set()
+    for r, k, rows_at, keys_at, masked in blocks():
+        if k not in ready:
+            ready.add(k)
+            prepare_keys(k)
+        if k == 0 and ("rows", r) not in ready:
+            ready.add(("rows", r))
+            prepare_rows(r)
+        waiting.append((r, k, rows_at, keys_at) + first(rows_at, keys_at, masked))
+        if len(waiting) > SKEW:
+            retire(*waiting.pop(0))
     for entry in waiting:
-        second(*entry)
+        retire(*entry)
 
     def unsort(place, carry):
         source = table[place]
@@ -270,8 +296,8 @@
         in_specs=[IN_SMEM, IN_VMEM, IN_VMEM],
         out_specs=IN_VMEM,
         scratch_shapes=[
-            pltpu.VMEM((ALL_ROWS, WIDTH), jnp.bfloat16),
-            pltpu.VMEM((ALL_KEYS, WIDTH), jnp.bfloat16),
+            pltpu.VMEM((ALL_ROWS, 2 * WIDTH), jnp.bfloat16),
+            pltpu.VMEM((ALL_KEYS, 2 * WIDTH), jnp.bfloat16),
         ],
         compiler_params=pltpu.CompilerParams(vmem_limit_bytes=20 * MIB),
         cost_estimate=pl.CostEstimate(

time: 139 us -> 134 us (0.964)
  Pallas kernels: 44.2 us -> 38.9 us
  blocking collectives: 38.3 us -> 34.7 us
  waiting for transfers between devices: 34.2 us -> 37.8 us
    pallas_call x1, Pallas kernels: 13.4 us -> 9.74 us  [stats_call(): pl.pallas_call(stats_kernel, out_shape=jax.ShapeDtypeStruct((2 * TILES, T...]
    all_to_all x1, blocking collectives: 38.3 us -> 34.7 us  [shards(): lax.all_to_all(outgoing, ALL, split_axis=0, concat_axis=0, tiled=True)]
    all_to_all x1, waiting for transfers between devices: 0.01 us -> 3.55 us  [shards(): lax.all_to_all(weighed, ALL, split_axis=0, concat_axis=0, tiled=True)]
    pallas_call x1, Pallas kernels: 24.5 us -> 22.9 us  [gradient_call(): pl.pallas_call(gradient_kernel, out_shape=(own, other), in_specs=[IN_SMEM...]
  transfers between devices with their start and end apart: 7 -> 7, of which waited for: 5 -> 6; matrix products, arithmetic and copies ran while one was open for 0% -> 0% of each run, Pallas kernels for 11% -> 9%
where the time goes in v4:
time: 134 us; the launch traced here: 133 us
  Pallas kernels  38.9 us (29%)
  waiting for transfers between devices  37.8 us (28%)
  blocking collectives  34.7 us (26%)
  starting transfers between devices  20 us (15%)
    all_to_all x1, blocking collectives, shards(): lax.all_to_all(outgoing, ALL, split_axis=0, concat_axis=0, tiled=True)  34.7 us
    all_to_all x1, waiting for transfers between devices, shards(): lax.all_to_all(scored, ALL, split_axis=0, concat_axis=0, tiled=True)  27.3 us
    pallas_call x1, Pallas kernels, gradient_call(): pl.pallas_call(gradient_kernel, out_shape=(own, other), in_specs=[IN_SMEM...  22.9 us
    all_to_all x1, starting transfers between devices, shards(): lax.all_to_all(scored, ALL, split_axis=0, concat_axis=0, tiled=True)  11.1 us
    pallas_call x1, Pallas kernels, stats_call(): pl.pallas_call(stats_kernel, out_shape=jax.ShapeDtypeStruct((2 * TILES, T...  9.74 us
    pallas_call x2, Pallas kernels, pack_call(): pl.pallas_call(kernel, out_shape=jax.ShapeDtypeStruct((DEVICES, height, W...  5.08 us
    all_to_all x1, starting transfers between devices, shards(): lax.all_to_all(weighed, ALL, split_axis=0, concat_axis=0, tiled=True)  4.77 us
    ppermute x3, waiting for transfers between devices, shards(): lax.ppermute(stats, ALL, around(k))  4.33 us
  transfers between devices with their start and end apart: 7, of which 6 were waited for; matrix products, arithmetic and copies ran while one was open for 0% of the time, Pallas kernels for 9%

profile of v4, /device:TPU:0, one launch (start us, length us, event | category | flops | bytes accessed | tf_op | source)
XLA Modules:
  0.0 133.4 jit_solution(9850120672556169686)
XLA Ops:
  0.6 2.7 %pack.2 = bf16[128,64,128]{2,1,0:T(8,128)(2,1)} custom-call(bf16[128,1024]{1,0:T(8,128)(2,1)} %rows.2, bf16[128,128]{1,0:T(8,128)(2,1)} %keys.1, bf16[128,128]{1,0:T(8,128)(2,1)} %values.1), custom_call_target="tpu_custom_call" | custom-call | tf_op jit(solution)/shard_map/outgoing/pack/pallas_call | solution.py:379
  3.3 11.1 %all-to-all-start = ((bf16[128,64,128]{2,1,0:T(8,128)(2,1)}), bf16[128,64,128]{2,1,0:T(8,128)(2,1)S(1)}, u32[]{:S(2)}, u32[]{:S(2)}) async-start(bf16[128,64,128]{2,1,0:T(8,128)(2,1)} %pack.2), calls=%async_computation | async-start | bytes 4194304 | tf_op jit(solution)/shard_map/exchange_in/all_to_all | solution.py:462
  14.4 2.4 %pack.3 = bf16[128,40,128]{2,1,0:T(8,128)(2,1)} custom-call(bf16[128,1024]{1,0:T(8,128)(2,1)} %rows.3, bf16[128,1024]{1,0:T(8,128)(2,1)} %forward.1), custom_call_target="tpu_custom_call" | custom-call | tf_op jit(solution)/shard_map/outgoing/pack/pallas_call | solution.py:379
  16.9 0.0 copy-start
  16.9 27.3 %all-to-all-done.scored = bf16[128,64,128]{2,1,0:T(8,128)(2,1)S(1)} async-done(((bf16[128,64,128]{2,1,0:T(8,128)(2,1)}), bf16[128,64,128]{2,1,0:T(8,128)(2,1)S(1)}, u32[]{:S(2)}, u32[]{:S(2)}) %all-to-all-start) | async-done | bytes 2097184 | tf_op jit(solution)/shard_map/exchange_in/all_to_all | solution.py:462
  44.1 1.1 slice.3
  45.3 0.0 collective-permute-start
  45.3 4.8 %all-to-all-start.1 = ((bf16[128,40,128]{2,1,0:T(8,128)(2,1)}), bf16[128,40,128]{2,1,0:T(8,128)(2,1)S(1)}, u32[]{:S(2)}, u32[]{:S(2)}) async-start(bf16[128,40,128]{2,1,0:T(8,128)(2,1)} %pack.3), calls=%async_computation.1 | async-start | bytes 2621440 | tf_op jit(solution)/shard_map/exchange_in/all_to_all | solution.py:464
  50.1 0.0 copy-done
  50.1 0.1 select_reduce_fusion
  50.2 0.1 pad_add_fusion.table
  50.3 0.0 collective-permute-done.other_half
  50.3 9.7 %softmax_totals.1.stats_0 = f32[16,512]{1,0:T(8,128)S(1)} custom-call(s32[131]{0:T(256)S(1)} %pad_add_fusion.table, bf16[128,64,128]{2,1,0:T(8,128)(2,1)S(1)} %all-to-all-done.scored, bf16[128,32,128]{2,1,0:T(8,128)(2,1)} %collective-permute-done.other_half), custom_call_target="tpu_custom_call" | custom-call | flops 2415919104 | bytes 4194304 | tf_op jit(solution)/shard_map/totals/softmax_totals/pallas_call | solution.py:293
  60.0 2.2 %collective-permute-start.3 = (f32[16,512]{1,0:T(8,128)S(1)}, f32[16,512]{1,0:T(8,128)S(1)}, u32[]{:S(2)}, u32[]{:S(2)}) collective-permute-start(f32[16,512]{1,0:T(8,128)S(1)} %softmax_totals.1.stats_0), channel_id=1, source_target_pairs={{0,96},{1,97},{2,98},{3,99},{4,100},{5,101},{6,102},{7,103},{8,104... | collective-permute-start | bytes 98312 | tf_op jit(solution)/shard_map/totals/ppermute | solution.py:468
  62.3 0.8 collective-permute-start.2
  63.1 0.9 collective-permute-start.1
  64.0 2.5 %collective-permute-done.3.stats_3 = f32[16,512]{1,0:T(8,128)S(1)} collective-permute-done((f32[16,512]{1,0:T(8,128)S(1)}, f32[16,512]{1,0:T(8,128)S(1)}, u32[]{:S(2)}, u32[]{:S(2)}) %collective-permute-start.3) | collective-permute-done | bytes 32800 | tf_op jit(solution)/shard_map/totals/ppermute | solution.py:468
  66.4 1.5 %collective-permute-done.2.stats_2 = f32[16,512]{1,0:T(8,128)S(1)} collective-permute-done((f32[16,512]{1,0:T(8,128)S(1)}, f32[16,512]{1,0:T(8,128)S(1)}, u32[]{:S(2)}, u32[]{:S(2)}) %collective-permute-start.2) | collective-permute-done | bytes 32800 | tf_op jit(solution)/shard_map/totals/ppermute | solution.py:468
  68.0 0.3 collective-permute-done.1.stats_1
  68.3 3.6 %all-to-all-done.1.weighed = bf16[128,40,128]{2,1,0:T(8,128)(2,1)S(1)} async-done(((bf16[128,40,128]{2,1,0:T(8,128)(2,1)}), bf16[128,40,128]{2,1,0:T(8,128)(2,1)S(1)}, u32[]{:S(2)}, u32[]{:S(2)}) %all-to-all-start.1) | async-done | bytes 1310752 | tf_op jit(solution)/shard_map/exchange_in/all_to_all | solution.py:464
  71.9 22.9 %gradients.1 = (bf16[128,64,128]{2,1,0:T(8,128)(2,1)S(1)}, bf16[128,32,128]{2,1,0:T(8,128)(2,1)S(1)}) custom-call(s32[131]{0:T(256)S(1)} %pad_add_fusion.table, bf16[128,64,128]{2,1,0:T(8,128)(2,1)S(1)} %all-to-all-done.scored, bf16[128,32,128]{2,1,0:T(8,128)(2,1)} %collective-permute-done.other_half, bf16[128,40,128]{2,1,0:T(8,128)(2,1)S(1)} %all-to-all-done.1.weighed, ...), custom_call_target="tpu_custom_call" | custom-call | flops 12079595520 | bytes 8388608 | tf_op jit(solution)/shard_map/gradients/gradients/pallas_call | solution.py:313
  94.8 0.1 collective-permute-start.4
  94.8 2.6 %collective-permute-done.4.received = bf16[128,32,128]{2,1,0:T(8,128)(2,1)S(1)} collective-permute-done((bf16[128,32,128]{2,1,0:T(8,128)(2,1)S(1)}, bf16[128,32,128]{2,1,0:T(8,128)(2,1)S(1)}, u32[]{:S(2)}, u32[]{:S(2)}) %collective-permute-start.4) | collective-permute-done | bytes 1048608 | tf_op jit(solution)/shard_map/exchange_out/ppermute | solution.py:475
  97.5 0.3 pair_sum.1
  97.8 34.7 %all_to_all.15.back = bf16[128,64,128]{2,1,0:T(8,128)(2,1)S(1)} all-to-all(bf16[128,64,128]{2,1,0:T(8,128)(2,1)S(1)} %pair_sum.1), channel_id=1, replica_groups=mesh['qrow'=32,'kcol'=4] {'qrow','kcol'}, dimensions={0} | all-to-all | bytes 4194304 | tf_op jit(solution)/shard_map/exchange_out/all_to_all | solution.py:477
  132.5 0.9 sums.1
Async XLA Ops:
  3.3 40.9 %all-to-all-start = ((bf16[128,64,128]{2,1,0:T(8,128)(2,1)}), bf16[128,64,128]{2,1,0:T(8,128)(2,1)S(1)}, u32[]{:S(2)}, u32[]{:S(2)}) async-start(bf16[128,64,128]{2,1,0:T(8,128)(2,1)} %pack.2), calls=%async_computation | async-start | bytes 4194304 | tf_op jit(solution)/shard_map/exchange_in/all_to_all | solution.py:462
  16.9 33.2 %copy-start = (s32[128]{0:T(128)S(1)}, s32[128]{0:T(128)}, u32[]{:S(2)}) copy-start(s32[128]{0:T(128)} %param.11) | copy-start | bytes 1540
  45.3 5.0 %collective-permute-start = (bf16[128,32,128]{2,1,0:T(8,128)(2,1)}, bf16[128,32,128]{2,1,0:T(8,128)(2,1)}, u32[]{:S(2)}, u32[]{:S(2)}) collective-permute-start(bf16[128,32,128]{2,1,0:T(8,128)(2,1)} %slice.3), channel_id=1, source_target_pairs={{0,1},{1,0},{2,3},{3,2},{4,5},{5,4},{6,7},{7,6},{8,9},{9,8},{10,11... | collective-permute-start | bytes 3145736 | tf_op jit(solution)/shard_map/exchange_in/ppermute | solution.py:465
  45.3 26.6 %all-to-all-start.1 = ((bf16[128,40,128]{2,1,0:T(8,128)(2,1)}), bf16[128,40,128]{2,1,0:T(8,128)(2,1)S(1)}, u32[]{:S(2)}, u32[]{:S(2)}) async-start(bf16[128,40,128]{2,1,0:T(8,128)(2,1)} %pack.3), calls=%async_computation.1 | async-start | bytes 2621440 | tf_op jit(solution)/shard_map/exchange_in/all_to_all | solution.py:464
  60.0 6.4 %collective-permute-start.3 = (f32[16,512]{1,0:T(8,128)S(1)}, f32[16,512]{1,0:T(8,128)S(1)}, u32[]{:S(2)}, u32[]{:S(2)}) collective-permute-start(f32[16,512]{1,0:T(8,128)S(1)} %softmax_totals.1.stats_0), channel_id=1, source_target_pairs={{0,96},{1,97},{2,98},{3,99},{4,100},{5,101},{6,102},{7,103},{8,104... | collective-permute-start | bytes 98312 | tf_op jit(solution)/shard_map/totals/ppermute | solution.py:468
  62.3 5.7 %collective-permute-start.2 = (f32[16,512]{1,0:T(8,128)S(1)}, f32[16,512]{1,0:T(8,128)S(1)}, u32[]{:S(2)}, u32[]{:S(2)}) collective-permute-start(f32[16,512]{1,0:T(8,128)S(1)} %softmax_totals.1.stats_0), channel_id=1, source_target_pairs={{0,64},{1,65},{2,66},{3,67},{4,68},{5,69},{6,70},{7,71},{8,72},{9,... | collective-permute-start | bytes 98312 | tf_op jit(solution)/shard_map/totals/ppermute | solution.py:468
  63.1 5.2 %collective-permute-start.1 = (f32[16,512]{1,0:T(8,128)S(1)}, f32[16,512]{1,0:T(8,128)S(1)}, u32[]{:S(2)}, u32[]{:S(2)}) collective-permute-start(f32[16,512]{1,0:T(8,128)S(1)} %softmax_totals.1.stats_0), channel_id=1, source_target_pairs={{0,32},{1,33},{2,34},{3,35},{4,36},{5,37},{6,38},{7,39},{8,40},{9,... | collective-permute-start | bytes 98312 | tf_op jit(solution)/shard_map/totals/ppermute | solution.py:468
  94.8 2.7 %collective-permute-start.4 = (bf16[128,32,128]{2,1,0:T(8,128)(2,1)S(1)}, bf16[128,32,128]{2,1,0:T(8,128)(2,1)S(1)}, u32[]{:S(2)}, u32[]{:S(2)}) collective-permute-start(bf16[128,32,128]{2,1,0:T(8,128)(2,1)S(1)} %get-tuple-element.20), channel_id=1, source_target_pairs={{0,1},{1,0},{2,3},{3,2},{4,5},{5,4},{6,7},{7,6},{8,9},{9,8},{10,11... | collective-permute-start | bytes 3145736 | tf_op jit(solution)/shard_map/exchange_out/ppermute | solution.py:475

commit v5 on v4

--- a/solution.py
+++ b/solution.py
@@ -72,7 +72,7 @@
             own_spot = pl.ds(pl.multiple_of(start + core * HALF, HALF), HALF)
             other_spot = pl.ds(pl.multiple_of(start + (1 - core) * HALF, HALF), HALF)
             own = scored[source, ROWS : ROWS + HALF]
-            other = other_half[source, 0:HALF]
+            other = other_half[source, ROWS : ROWS + HALF]
             key[own_spot, 0:WIDTH] = own
             key[own_spot, WIDTH:] = own
             key[other_spot, 0:WIDTH] = other
@@ -82,27 +82,33 @@
     state = {}
 
     def absorb(r, first, masked):
-        scores = contract(key[first : first + CHUNK], query[r * TILE : (r + 1) * TILE], 1, 1)
+        begin = HALF_TILE if masked and first % TILE >= HALF_TILE else 0
+        rows = slice(r * TILE + begin, (r + 1) * TILE)
+        scores = contract(key[first : first + CHUNK], query[rows], 1, 1)
         if masked:
             inside = first - r * TILE
-            scores = jnp.where(allowed[inside : inside + CHUNK], scores, NEGATIVE)
-        scores = scores.reshape(CHUNK // SUBLANES, SUBLANES, TILE)
-        chunk_peak = jnp.max(scores, axis=0)
-        if r not in state:
-            raised = chunk_peak
-            state[r] = raised, jnp.sum(jnp.exp2(scores - raised[None]), axis=0)
-            return
-        highest, summed = state[r]
-        raised = jnp.maximum(highest, chunk_peak)
-        summed = summed * jnp.exp2(highest - raised)
-        state[r] = raised, summed + jnp.sum(jnp.exp2(scores - raised[None]), axis=0)
+            scores = jnp.where(allowed[inside : inside + CHUNK, begin:], scores, NEGATIVE)
+        scores = scores.reshape(CHUNK // SUBLANES, SUBLANES, TILE - begin)
+        for n in range(begin // HALF_TILE, 2):
+            part = scores[..., n * HALF_TILE - begin : (n + 1) * HALF_TILE - begin]
+            raised = jnp.max(part, axis=0)
+            if (r, n) in state:
+                highest, summed = state[r, n]
+                raised = jnp.maximum(highest, raised)
+                summed = summed * jnp.exp2(highest - raised)
+                summed = summed + jnp.sum(jnp.exp2(part - raised[None]), axis=0)
+            else:
+                summed = jnp.sum(jnp.exp2(part - raised[None]), axis=0)
+            state[r, n] = raised, summed
 
     def finish(r):
-        highest, summed = state.pop(r)
-        row_peak = jnp.max(highest, axis=0, keepdims=True)
-        row_total = jnp.sum(summed * jnp.exp2(highest - row_peak), axis=0, keepdims=True)
-        stats[r : r + 1] = row_peak
-        stats[r + TILES : r + TILES + 1] = row_total
+        for n in range(2):
+            highest, summed = state.pop((r, n))
+            row_peak = jnp.max(highest, axis=0, keepdims=True)
+            row_total = jnp.sum(summed * jnp.exp2(highest - row_peak), axis=0, keepdims=True)
+            lanes = slice(n * HALF_TILE, (n + 1) * HALF_TILE)
+            stats[r : r + 1, lanes] = row_peak
+            stats[r + TILES : r + TILES + 1, lanes] = row_total
 
     for first in range(0, ALL_KEYS, CHUNK):
         if first % TILE == 0:
@@ -189,9 +195,9 @@
             own_spot = pl.ds(pl.multiple_of(start + core * HALF, HALF), HALF)
             other_spot = pl.ds(pl.multiple_of(start + (1 - core) * HALF, HALF), HALF)
             key[own_spot, 0:WIDTH] = scored[source, ROWS : ROWS + HALF]
-            key[other_spot, 0:WIDTH] = other_half[source, 0:HALF]
+            key[other_spot, 0:WIDTH] = other_half[source, ROWS : ROWS + HALF]
             value[own_spot, 0:WIDTH] = scored[source, ROWS + HALF : ROWS + 2 * HALF]
-            value[other_spot, 0:WIDTH] = other_half[source, HALF : 2 * HALF]
+            value[other_spot, 0:WIDTH] = other_half[source, ROWS + HALF :]
 
     def first(rows_at, keys_at, masked):
         scores = contract(query[rows_at], key[keys_at], 1, 1)
@@ -232,6 +238,15 @@
             here = slice(k * TILE + n * HALF_TILE, k * TILE + (n + 1) * HALF_TILE)
             key_sorted[here] = (key_sums.pop((k, n)) * SCALE).astype(jnp.bfloat16).T
             value_sorted[here] = value_sums.pop((k, n)).astype(jnp.bfloat16).T
+            for s in range(n * SPAN // 2, (n + 1) * SPAN // 2):
+                source = table[k * SPAN + s]
+                start = k * TILE + s * KEY_TOKENS
+                own_spot = pl.ds(pl.multiple_of(start + core * HALF, HALF), HALF)
+                other_spot = pl.ds(pl.multiple_of(start + (1 - core) * HALF, HALF), HALF)
+                own_grad[source, ROWS : ROWS + HALF] = key_sorted[own_spot]
+                own_grad[source, ROWS + HALF :] = value_sorted[own_spot]
+                other_grad[source, 0:HALF] = key_sorted[other_spot]
+                other_grad[source, HALF:] = value_sorted[other_spot]
 
     def blocks():
         for k in range(TILES):
@@ -270,18 +285,6 @@
             retire(*waiting.pop(0))
     for entry in waiting:
         retire(*entry)
-
-    def unsort(place, carry):
-        source = table[place]
-        first = pl.ds(pl.multiple_of(place * KEY_TOKENS + core * HALF, HALF), HALF)
-        second = pl.ds(pl.multiple_of(place * KEY_TOKENS + (1 - core) * HALF, HALF), HALF)
-        own_grad[source, ROWS : ROWS + HALF] = key_sorted[first]
-        own_grad[source, ROWS + HALF :] = value_sorted[first]
-        other_grad[source, 0:HALF] = key_sorted[second]
-        other_grad[source, HALF:] = value_sorted[second]
-        return carry
-
-    lax.fori_loop(0, PLACES, unsort, 0, unroll=8)
 
 
 IN_VMEM = pl.BlockSpec(memory_space=pltpu.VMEM)
@@ -462,7 +465,7 @@
         scored = lax.all_to_all(scored, ALL, split_axis=0, concat_axis=0, tiled=True)
         scored, weighed = lax.optimization_barrier((scored, weighed))
         weighed = lax.all_to_all(weighed, ALL, split_axis=0, concat_axis=0, tiled=True)
-        other_half = lax.ppermute(scored[:, ROWS:], ALL, swap)
+        other_half = lax.ppermute(scored, ALL, swap)
     with jax.named_scope("totals"):
         stats = stats_call(table, scored, other_half)
         all_stats = [stats] + [lax.ppermute(stats, ALL, around(k)) for k in range(1, KEY_GROUPS)]

time: 134 us -> 133 us (level)
    all_to_all x1, waiting for transfers between devices: 3.55 us -> 8.31 us  [shards(): lax.all_to_all(weighed, ALL, split_axis=0, concat_axis=0, tiled=True)]
    ppermute x3, waiting for transfers between devices: 4.33 us -> 0.01 us  [shards(): lax.ppermute(stats, ALL, around(k))]
  transfers between devices with their start and end apart: 7 -> 7, of which waited for: 6 -> 3; matrix products, arithmetic and copies ran while one was open for 0% -> 0% of each run, Pallas kernels for 9% -> 9%
where the time goes in v5:
time: 133 us; the launch traced here: 132 us
  Pallas kernels  38.7 us (29%)
  waiting for transfers between devices  38.2 us (29%)
  blocking collectives  34.4 us (26%)
  starting transfers between devices  20 us (15%)
    all_to_all x1, blocking collectives, shards(): lax.all_to_all(outgoing, ALL, split_axis=0, concat_axis=0, tiled=True)  34.4 us
    all_to_all x1, waiting for transfers between devices, shards(): lax.all_to_all(scored, ALL, split_axis=0, concat_axis=0, tiled=True)  27.3 us
    pallas_call x1, Pallas kernels, gradient_call(): pl.pallas_call(gradient_kernel, out_shape=(own, other), in_specs=[IN_SMEM...  23.1 us
    all_to_all x1, starting transfers between devices, shards(): lax.all_to_all(scored, ALL, split_axis=0, concat_axis=0, tiled=True)  11.1 us
    pallas_call x1, Pallas kernels, stats_call(): pl.pallas_call(stats_kernel, out_shape=jax.ShapeDtypeStruct((2 * TILES, T...  9.3 us
    all_to_all x1, waiting for transfers between devices, shards(): lax.all_to_all(weighed, ALL, split_axis=0, concat_axis=0, tiled=True)  8.31 us
    pallas_call x2, Pallas kernels, pack_call(): pl.pallas_call(kernel, out_shape=jax.ShapeDtypeStruct((DEVICES, height, W...  5.08 us
    all_to_all x1, starting transfers between devices, shards(): lax.all_to_all(weighed, ALL, split_axis=0, concat_axis=0, tiled=True)  4.77 us
  transfers between devices with their start and end apart: 7, of which 3 were waited for; matrix products, arithmetic and copies ran while one was open for 0% of the time, Pallas kernels for 9%

profile of v5, /device:TPU:0, one launch (start us, length us, event | category | flops | bytes accessed | tf_op | source)
XLA Modules:
  0.0 132.1 jit_solution(2308759997117935778)
XLA Ops:
  0.6 2.7 %pack.2 = bf16[128,64,128]{2,1,0:T(8,128)(2,1)} custom-call(bf16[128,1024]{1,0:T(8,128)(2,1)} %rows.2, bf16[128,128]{1,0:T(8,128)(2,1)} %keys.1, bf16[128,128]{1,0:T(8,128)(2,1)} %values.1), custom_call_target="tpu_custom_call" | custom-call | tf_op jit(solution)/shard_map/outgoing/pack/pallas_call | solution.py:382
  3.3 11.1 %all-to-all-start = ((bf16[128,64,128]{2,1,0:T(8,128)(2,1)}), bf16[128,64,128]{2,1,0:T(8,128)(2,1)S(1)}, u32[]{:S(2)}, u32[]{:S(2)}) async-start(bf16[128,64,128]{2,1,0:T(8,128)(2,1)} %pack.2), calls=%async_computation | async-start | bytes 4194304 | tf_op jit(solution)/shard_map/exchange_in/all_to_all | solution.py:465
  14.4 0.0 copy-start
  14.4 2.4 %pack.3 = bf16[128,40,128]{2,1,0:T(8,128)(2,1)} custom-call(bf16[128,1024]{1,0:T(8,128)(2,1)} %rows.3, bf16[128,1024]{1,0:T(8,128)(2,1)} %forward.1), custom_call_target="tpu_custom_call" | custom-call | tf_op jit(solution)/shard_map/outgoing/pack/pallas_call | solution.py:382
  16.9 27.3 %all-to-all-done.scored = bf16[128,64,128]{2,1,0:T(8,128)(2,1)S(1)} async-done(((bf16[128,64,128]{2,1,0:T(8,128)(2,1)}), bf16[128,64,128]{2,1,0:T(8,128)(2,1)S(1)}, u32[]{:S(2)}, u32[]{:S(2)}) %all-to-all-start) | async-done | bytes 2097184 | tf_op jit(solution)/shard_map/exchange_in/all_to_all | solution.py:465
  44.1 0.0 collective-permute-start
  44.1 4.8 %all-to-all-start.1 = ((bf16[128,40,128]{2,1,0:T(8,128)(2,1)}), bf16[128,40,128]{2,1,0:T(8,128)(2,1)S(1)}, u32[]{:S(2)}, u32[]{:S(2)}) async-start(bf16[128,40,128]{2,1,0:T(8,128)(2,1)} %pack.3), calls=%async_computation.1 | async-start | bytes 2621440 | tf_op jit(solution)/shard_map/exchange_in/all_to_all | solution.py:467
  49.0 0.0 copy-done
  49.0 0.1 select_reduce_fusion
  49.1 0.1 pad_add_fusion.table
  49.2 0.0 collective-permute-done.other_half
  49.2 9.3 %softmax_totals.1.stats_0 = f32[16,512]{1,0:T(8,128)S(1)} custom-call(s32[131]{0:T(256)S(1)} %pad_add_fusion.table, bf16[128,64,128]{2,1,0:T(8,128)(2,1)S(1)} %all-to-all-done.scored, bf16[128,64,128]{2,1,0:T(8,128)(2,1)} %collective-permute-done.other_half), custom_call_target="tpu_custom_call" | custom-call | flops 2415919104 | bytes 4194304 | tf_op jit(solution)/shard_map/totals/softmax_totals/pallas_call | solution.py:296
  58.5 2.2 %collective-permute-start.3 = (f32[16,512]{1,0:T(8,128)S(1)}, f32[16,512]{1,0:T(8,128)S(1)}, u32[]{:S(2)}, u32[]{:S(2)}) collective-permute-start(f32[16,512]{1,0:T(8,128)S(1)} %softmax_totals.1.stats_0), channel_id=1, source_target_pairs={{0,96},{1,97},{2,98},{3,99},{4,100},{5,101},{6,102},{7,103},{8,104... | collective-permute-start | bytes 98312 | tf_op jit(solution)/shard_map/totals/ppermute | solution.py:471
  60.7 0.9 collective-permute-start.2
  61.6 0.9 collective-permute-start.1
  62.4 8.3 %all-to-all-done.1.weighed = bf16[128,40,128]{2,1,0:T(8,128)(2,1)S(1)} async-done(((bf16[128,40,128]{2,1,0:T(8,128)(2,1)}), bf16[128,40,128]{2,1,0:T(8,128)(2,1)S(1)}, u32[]{:S(2)}, u32[]{:S(2)}) %all-to-all-start.1) | async-done | bytes 1310752 | tf_op jit(solution)/shard_map/exchange_in/all_to_all | solution.py:467
  70.7 0.0 collective-permute-done.3.stats_3
  70.7 0.0 collective-permute-done.2.stats_2
  70.7 0.0 collective-permute-done.1.stats_1
  70.7 23.1 %gradients.1 = (bf16[128,64,128]{2,1,0:T(8,128)(2,1)S(1)}, bf16[128,32,128]{2,1,0:T(8,128)(2,1)S(1)}) custom-call(s32[131]{0:T(256)S(1)} %pad_add_fusion.table, bf16[128,64,128]{2,1,0:T(8,128)(2,1)S(1)} %all-to-all-done.scored, bf16[128,64,128]{2,1,0:T(8,128)(2,1)} %collective-permute-done.other_half, bf16[128,40,128]{2,1,0:T(8,128)(2,1)S(1)} %all-to-all-done.1.weighed, ...), custom_call_target="tpu_custom_call" | custom-call | flops 12079595520 | bytes 8388608 | tf_op jit(solution)/shard_map/gradients/gradients/pallas_call | solution.py:316
  93.8 0.1 collective-permute-start.4
  93.9 2.6 %collective-permute-done.4.received = bf16[128,32,128]{2,1,0:T(8,128)(2,1)S(1)} collective-permute-done((bf16[128,32,128]{2,1,0:T(8,128)(2,1)S(1)}, bf16[128,32,128]{2,1,0:T(8,128)(2,1)S(1)}, u32[]{:S(2)}, u32[]{:S(2)}) %collective-permute-start.4) | collective-permute-done | bytes 1048608 | tf_op jit(solution)/shard_map/exchange_out/ppermute | solution.py:478
  96.5 0.3 pair_sum.1
  96.9 34.4 %all_to_all.15.back = bf16[128,64,128]{2,1,0:T(8,128)(2,1)S(1)} all-to-all(bf16[128,64,128]{2,1,0:T(8,128)(2,1)S(1)} %pair_sum.1), channel_id=1, replica_groups=mesh['qrow'=32,'kcol'=4] {'qrow','kcol'}, dimensions={0} | all-to-all | bytes 4194304 | tf_op jit(solution)/shard_map/exchange_out/all_to_all | solution.py:480
  131.2 0.9 sums.1
Async XLA Ops:
  3.3 40.9 %all-to-all-start = ((bf16[128,64,128]{2,1,0:T(8,128)(2,1)}), bf16[128,64,128]{2,1,0:T(8,128)(2,1)S(1)}, u32[]{:S(2)}, u32[]{:S(2)}) async-start(bf16[128,64,128]{2,1,0:T(8,128)(2,1)} %pack.2), calls=%async_computation | async-start | bytes 4194304 | tf_op jit(solution)/shard_map/exchange_in/all_to_all | solution.py:465
  14.4 34.5 %copy-start = (s32[128]{0:T(128)S(1)}, s32[128]{0:T(128)}, u32[]{:S(2)}) copy-start(s32[128]{0:T(128)} %param.11) | copy-start | bytes 1540
  44.1 5.0 %collective-permute-start = (bf16[128,64,128]{2,1,0:T(8,128)(2,1)S(1)}, bf16[128,64,128]{2,1,0:T(8,128)(2,1)}, u32[]{:S(2)}, u32[]{:S(2)}) collective-permute-start(bf16[128,64,128]{2,1,0:T(8,128)(2,1)S(1)} %all-to-all-done.scored), channel_id=1, source_target_pairs={{0,1},{1,0},{2,3},{3,2},{4,5},{5,4},{6,7},{7,6},{8,9},{9,8},{10,11... | collective-permute-start | bytes 6291464 | tf_op jit(solution)/shard_map/exchange_in/ppermute | solution.py:468
  44.1 26.6 %all-to-all-start.1 = ((bf16[128,40,128]{2,1,0:T(8,128)(2,1)}), bf16[128,40,128]{2,1,0:T(8,128)(2,1)S(1)}, u32[]{:S(2)}, u32[]{:S(2)}) async-start(bf16[128,40,128]{2,1,0:T(8,128)(2,1)} %pack.3), calls=%async_computation.1 | async-start | bytes 2621440 | tf_op jit(solution)/shard_map/exchange_in/all_to_all | solution.py:467
  58.5 12.3 %collective-permute-start.3 = (f32[16,512]{1,0:T(8,128)S(1)}, f32[16,512]{1,0:T(8,128)S(1)}, u32[]{:S(2)}, u32[]{:S(2)}) collective-permute-start(f32[16,512]{1,0:T(8,128)S(1)} %softmax_totals.1.stats_0), channel_id=1, source_target_pairs={{0,96},{1,97},{2,98},{3,99},{4,100},{5,101},{6,102},{7,103},{8,104... | collective-permute-start | bytes 98312 | tf_op jit(solution)/shard_map/totals/ppermute | solution.py:471
  60.7 10.0 %collective-permute-start.2 = (f32[16,512]{1,0:T(8,128)S(1)}, f32[16,512]{1,0:T(8,128)S(1)}, u32[]{:S(2)}, u32[]{:S(2)}) collective-permute-start(f32[16,512]{1,0:T(8,128)S(1)} %softmax_totals.1.stats_0), channel_id=1, source_target_pairs={{0,64},{1,65},{2,66},{3,67},{4,68},{5,69},{6,70},{7,71},{8,72},{9,... | collective-permute-start | bytes 98312 | tf_op jit(solution)/shard_map/totals/ppermute | solution.py:471
  61.6 9.2 %collective-permute-start.1 = (f32[16,512]{1,0:T(8,128)S(1)}, f32[16,512]{1,0:T(8,128)S(1)}, u32[]{:S(2)}, u32[]{:S(2)}) collective-permute-start(f32[16,512]{1,0:T(8,128)S(1)} %softmax_totals.1.stats_0), channel_id=1, source_target_pairs={{0,32},{1,33},{2,34},{3,35},{4,36},{5,37},{6,38},{7,39},{8,40},{9,... | collective-permute-start | bytes 98312 | tf_op jit(solution)/shard_map/totals/ppermute | solution.py:471
  93.8 2.7 %collective-permute-start.4 = (bf16[128,32,128]{2,1,0:T(8,128)(2,1)S(1)}, bf16[128,32,128]{2,1,0:T(8,128)(2,1)S(1)}, u32[]{:S(2)}, u32[]{:S(2)}) collective-permute-start(bf16[128,32,128]{2,1,0:T(8,128)(2,1)S(1)} %get-tuple-element.20), channel_id=1, source_target_pairs={{0,1},{1,0},{2,3},{3,2},{4,5},{5,4},{6,7},{7,6},{8,9},{9,8},{10,11... | collective-permute-start | bytes 3145736 | tf_op jit(solution)/shard_map/exchange_out/ppermute | solution.py:478

commit v6 on v5

--- a/solution.py
+++ b/solution.py
@@ -124,7 +124,7 @@
 def gradient_kernel(
     table,
     scored,
-    other_half,
+    swapped,
     weighed,
     stats_0,
     stats_1,
@@ -141,7 +141,11 @@
     logs,
     key_sorted,
     value_sorted,
+    other_half,
+    arrived,
 ):
+    fetch = pltpu.make_async_copy(swapped.at[:, pl.ds(ROWS, 2 * HALF)], other_half, arrived)
+    fetch.start()
     key_group, row_group, core = table[PLACES], table[PLACES + 1], table[PLACES + 2]
     lane = lax.broadcasted_iota(jnp.int32, (TILE, WIDTH), 1)
     row_token = lax.broadcasted_iota(jnp.int32, (ROWS, WIDTH), 0) % QUERY_TOKENS
@@ -195,9 +199,9 @@
             own_spot = pl.ds(pl.multiple_of(start + core * HALF, HALF), HALF)
             other_spot = pl.ds(pl.multiple_of(start + (1 - core) * HALF, HALF), HALF)
             key[own_spot, 0:WIDTH] = scored[source, ROWS : ROWS + HALF]
-            key[other_spot, 0:WIDTH] = other_half[source, ROWS : ROWS + HALF]
+            key[other_spot, 0:WIDTH] = other_half[source, 0:HALF]
             value[own_spot, 0:WIDTH] = scored[source, ROWS + HALF : ROWS + 2 * HALF]
-            value[other_spot, 0:WIDTH] = other_half[source, ROWS + HALF :]
+            value[other_spot, 0:WIDTH] = other_half[source, HALF:]
 
     def first(rows_at, keys_at, masked):
         scores = contract(query[rows_at], key[keys_at], 1, 1)
@@ -272,7 +276,9 @@
             finish_keys(k)
 
     waiting = []
-    ready = set()
+    ready = {("rows", 0)}
+    prepare_rows(0)
+    fetch.wait()
     for r, k, rows_at, keys_at, masked in blocks():
         if k not in ready:
             ready.add(k)
@@ -316,7 +322,7 @@
     return pl.pallas_call(
         gradient_kernel,
         out_shape=(own, other),
-        in_specs=[IN_SMEM] + [IN_VMEM] * 7,
+        in_specs=[IN_SMEM, IN_VMEM, pl.BlockSpec(memory_space=pl.ANY)] + [IN_VMEM] * 5,
         out_specs=(IN_VMEM,) * 2,
         scratch_shapes=[
             pltpu.VMEM((ALL_ROWS, 2 * WIDTH), jnp.bfloat16),
@@ -328,6 +334,8 @@
             pltpu.VMEM((TILE, WIDTH), jnp.float32),
             pltpu.VMEM((ALL_KEYS, WIDTH), jnp.bfloat16),
             pltpu.VMEM((ALL_KEYS, WIDTH), jnp.bfloat16),
+            pltpu.VMEM((PLACES, 2 * HALF, WIDTH), jnp.bfloat16),
+            pltpu.SemaphoreType.DMA,
         ],
         compiler_params=pltpu.CompilerParams(vmem_limit_bytes=32 * MIB),
         cost_estimate=pl.CostEstimate(

time: 133 us -> 133 us (level)
  no operation moved by 1% of the time
where the time goes in v6:
time: 133 us; the launch traced here: 132 us
  Pallas kernels  38.6 us (29%)
  waiting for transfers between devices  38.2 us (29%)
  blocking collectives  34.4 us (26%)
  starting transfers between devices  20 us (15%)
    all_to_all x1, blocking collectives, shards(): lax.all_to_all(outgoing, ALL, split_axis=0, concat_axis=0, tiled=True)  34.4 us
    all_to_all x1, waiting for transfers between devices, shards(): lax.all_to_all(scored, ALL, split_axis=0, concat_axis=0, tiled=True)  27.3 us
    pallas_call x1, Pallas kernels, gradient_call(): pl.pallas_call(gradient_kernel, out_shape=(own, other), in_specs=[IN_SMEM...  23 us
    all_to_all x1, starting transfers between devices, shards(): lax.all_to_all(scored, ALL, split_axis=0, concat_axis=0, tiled=True)  11.1 us
    pallas_call x1, Pallas kernels, stats_call(): pl.pallas_call(stats_kernel, out_shape=jax.ShapeDtypeStruct((2 * TILES, T...  9.31 us
    all_to_all x1, waiting for transfers between devices, shards(): lax.all_to_all(weighed, ALL, split_axis=0, concat_axis=0, tiled=True)  8.31 us
    pallas_call x2, Pallas kernels, pack_call(): pl.pallas_call(kernel, out_shape=jax.ShapeDtypeStruct((DEVICES, height, W...  5.08 us
    all_to_all x1, starting transfers between devices, shards(): lax.all_to_all(weighed, ALL, split_axis=0, concat_axis=0, tiled=True)  4.77 us
  transfers between devices with their start and end apart: 7, of which 3 were waited for; matrix products, arithmetic and copies ran while one was open for 0% of the time, Pallas kernels for 9%

profile of v6, /device:TPU:0, one launch (start us, length us, event | category | flops | bytes accessed | tf_op | source)
XLA Modules:
  0.0 132.1 jit_solution(16242542578973679956)
XLA Ops:
  0.6 2.7 %pack.2 = bf16[128,64,128]{2,1,0:T(8,128)(2,1)} custom-call(bf16[128,1024]{1,0:T(8,128)(2,1)} %rows.2, bf16[128,128]{1,0:T(8,128)(2,1)} %keys.1, bf16[128,128]{1,0:T(8,128)(2,1)} %values.1), custom_call_target="tpu_custom_call" | custom-call | tf_op jit(solution)/shard_map/outgoing/pack/pallas_call | solution.py:390
  3.3 11.1 %all-to-all-start = ((bf16[128,64,128]{2,1,0:T(8,128)(2,1)}), bf16[128,64,128]{2,1,0:T(8,128)(2,1)S(1)}, u32[]{:S(2)}, u32[]{:S(2)}) async-start(bf16[128,64,128]{2,1,0:T(8,128)(2,1)} %pack.2), calls=%async_computation | async-start | bytes 4194304 | tf_op jit(solution)/shard_map/exchange_in/all_to_all | solution.py:473
  14.4 0.0 copy-start
  14.4 2.4 %pack.3 = bf16[128,40,128]{2,1,0:T(8,128)(2,1)} custom-call(bf16[128,1024]{1,0:T(8,128)(2,1)} %rows.3, bf16[128,1024]{1,0:T(8,128)(2,1)} %forward.1), custom_call_target="tpu_custom_call" | custom-call | tf_op jit(solution)/shard_map/outgoing/pack/pallas_call | solution.py:390
  16.9 27.3 %all-to-all-done.scored = bf16[128,64,128]{2,1,0:T(8,128)(2,1)S(1)} async-done(((bf16[128,64,128]{2,1,0:T(8,128)(2,1)}), bf16[128,64,128]{2,1,0:T(8,128)(2,1)S(1)}, u32[]{:S(2)}, u32[]{:S(2)}) %all-to-all-start) | async-done | bytes 2097184 | tf_op jit(solution)/shard_map/exchange_in/all_to_all | solution.py:473
  44.1 0.0 collective-permute-start
  44.1 4.8 %all-to-all-start.1 = ((bf16[128,40,128]{2,1,0:T(8,128)(2,1)}), bf16[128,40,128]{2,1,0:T(8,128)(2,1)S(1)}, u32[]{:S(2)}, u32[]{:S(2)}) async-start(bf16[128,40,128]{2,1,0:T(8,128)(2,1)} %pack.3), calls=%async_computation.1 | async-start | bytes 2621440 | tf_op jit(solution)/shard_map/exchange_in/all_to_all | solution.py:475
  49.0 0.0 copy-done
  49.0 0.1 select_reduce_fusion
  49.1 0.1 pad_add_fusion.table
  49.2 0.0 collective-permute-done.other_half.swapped
  49.2 9.3 %softmax_totals.1.stats_0 = f32[16,512]{1,0:T(8,128)S(1)} custom-call(s32[131]{0:T(256)S(1)} %pad_add_fusion.table, bf16[128,64,128]{2,1,0:T(8,128)(2,1)S(1)} %all-to-all-done.scored, bf16[128,64,128]{2,1,0:T(8,128)(2,1)} %collective-permute-done.other_half.swapped), custom_call_target="tpu_custom_call" | custom-call | flops 2415919104 | bytes 4194304 | tf_op jit(solution)/shard_map/totals/softmax_totals/pallas_call | solution.py:302
  58.5 2.2 %collective-permute-start.3 = (f32[16,512]{1,0:T(8,128)S(1)}, f32[16,512]{1,0:T(8,128)S(1)}, u32[]{:S(2)}, u32[]{:S(2)}) collective-permute-start(f32[16,512]{1,0:T(8,128)S(1)} %softmax_totals.1.stats_0), channel_id=1, source_target_pairs={{0,96},{1,97},{2,98},{3,99},{4,100},{5,101},{6,102},{7,103},{8,104... | collective-permute-start | bytes 98312 | tf_op jit(solution)/shard_map/totals/ppermute | solution.py:479
  60.7 0.9 collective-permute-start.2
  61.6 0.9 collective-permute-start.1
  62.4 8.3 %all-to-all-done.1.weighed = bf16[128,40,128]{2,1,0:T(8,128)(2,1)S(1)} async-done(((bf16[128,40,128]{2,1,0:T(8,128)(2,1)}), bf16[128,40,128]{2,1,0:T(8,128)(2,1)S(1)}, u32[]{:S(2)}, u32[]{:S(2)}) %all-to-all-start.1) | async-done | bytes 1310752 | tf_op jit(solution)/shard_map/exchange_in/all_to_all | solution.py:475
  70.7 0.0 collective-permute-done.3.stats_3
  70.7 0.0 collective-permute-done.2.stats_2
  70.7 0.0 collective-permute-done.1.stats_1
  70.7 23.0 %gradients.1 = (bf16[128,64,128]{2,1,0:T(8,128)(2,1)S(1)}, bf16[128,32,128]{2,1,0:T(8,128)(2,1)S(1)}) custom-call(s32[131]{0:T(256)S(1)} %pad_add_fusion.table, bf16[128,64,128]{2,1,0:T(8,128)(2,1)S(1)} %all-to-all-done.scored, bf16[128,64,128]{2,1,0:T(8,128)(2,1)} %collective-permute-done.other_half.swapped, ...), custom_call_target="tpu_custom_call" | custom-call | flops 12079595520 | bytes 8388608 | tf_op jit(solution)/shard_map/gradients/gradients/pallas_call | solution.py:322
  93.7 0.1 collective-permute-start.4
  93.8 2.6 %collective-permute-done.4.received = bf16[128,32,128]{2,1,0:T(8,128)(2,1)S(1)} collective-permute-done((bf16[128,32,128]{2,1,0:T(8,128)(2,1)S(1)}, bf16[128,32,128]{2,1,0:T(8,128)(2,1)S(1)}, u32[]{:S(2)}, u32[]{:S(2)}) %collective-permute-start.4) | collective-permute-done | bytes 1048608 | tf_op jit(solution)/shard_map/exchange_out/ppermute | solution.py:486
  96.5 0.3 pair_sum.1
  96.8 34.4 %all_to_all.15.back = bf16[128,64,128]{2,1,0:T(8,128)(2,1)S(1)} all-to-all(bf16[128,64,128]{2,1,0:T(8,128)(2,1)S(1)} %pair_sum.1), channel_id=1, replica_groups=mesh['qrow'=32,'kcol'=4] {'qrow','kcol'}, dimensions={0} | all-to-all | bytes 4194304 | tf_op jit(solution)/shard_map/exchange_out/all_to_all | solution.py:488
  131.2 0.9 sums.1
Async XLA Ops:
  3.3 40.9 %all-to-all-start = ((bf16[128,64,128]{2,1,0:T(8,128)(2,1)}), bf16[128,64,128]{2,1,0:T(8,128)(2,1)S(1)}, u32[]{:S(2)}, u32[]{:S(2)}) async-start(bf16[128,64,128]{2,1,0:T(8,128)(2,1)} %pack.2), calls=%async_computation | async-start | bytes 4194304 | tf_op jit(solution)/shard_map/exchange_in/all_to_all | solution.py:473
  14.4 34.5 %copy-start = (s32[128]{0:T(128)S(1)}, s32[128]{0:T(128)}, u32[]{:S(2)}) copy-start(s32[128]{0:T(128)} %param.11) | copy-start | bytes 1540
  44.1 5.0 %collective-permute-start = (bf16[128,64,128]{2,1,0:T(8,128)(2,1)S(1)}, bf16[128,64,128]{2,1,0:T(8,128)(2,1)}, u32[]{:S(2)}, u32[]{:S(2)}) collective-permute-start(bf16[128,64,128]{2,1,0:T(8,128)(2,1)S(1)} %all-to-all-done.scored), channel_id=1, source_target_pairs={{0,1},{1,0},{2,3},{3,2},{4,5},{5,4},{6,7},{7,6},{8,9},{9,8},{10,11... | collective-permute-start | bytes 6291464 | tf_op jit(solution)/shard_map/exchange_in/ppermute | solution.py:476
  44.1 26.6 %all-to-all-start.1 = ((bf16[128,40,128]{2,1,0:T(8,128)(2,1)}), bf16[128,40,128]{2,1,0:T(8,128)(2,1)S(1)}, u32[]{:S(2)}, u32[]{:S(2)}) async-start(bf16[128,40,128]{2,1,0:T(8,128)(2,1)} %pack.3), calls=%async_computation.1 | async-start | bytes 2621440 | tf_op jit(solution)/shard_map/exchange_in/all_to_all | solution.py:475
  58.5 12.3 %collective-permute-start.3 = (f32[16,512]{1,0:T(8,128)S(1)}, f32[16,512]{1,0:T(8,128)S(1)}, u32[]{:S(2)}, u32[]{:S(2)}) collective-permute-start(f32[16,512]{1,0:T(8,128)S(1)} %softmax_totals.1.stats_0), channel_id=1, source_target_pairs={{0,96},{1,97},{2,98},{3,99},{4,100},{5,101},{6,102},{7,103},{8,104... | collective-permute-start | bytes 98312 | tf_op jit(solution)/shard_map/totals/ppermute | solution.py:479
  60.7 10.0 %collective-permute-start.2 = (f32[16,512]{1,0:T(8,128)S(1)}, f32[16,512]{1,0:T(8,128)S(1)}, u32[]{:S(2)}, u32[]{:S(2)}) collective-permute-start(f32[16,512]{1,0:T(8,128)S(1)} %softmax_totals.1.stats_0), channel_id=1, source_target_pairs={{0,64},{1,65},{2,66},{3,67},{4,68},{5,69},{6,70},{7,71},{8,72},{9,... | collective-permute-start | bytes 98312 | tf_op jit(solution)/shard_map/totals/ppermute | solution.py:479
  61.6 9.2 %collective-permute-start.1 = (f32[16,512]{1,0:T(8,128)S(1)}, f32[16,512]{1,0:T(8,128)S(1)}, u32[]{:S(2)}, u32[]{:S(2)}) collective-permute-start(f32[16,512]{1,0:T(8,128)S(1)} %softmax_totals.1.stats_0), channel_id=1, source_target_pairs={{0,32},{1,33},{2,34},{3,35},{4,36},{5,37},{6,38},{7,39},{8,40},{9,... | collective-permute-start | bytes 98312 | tf_op jit(solution)/shard_map/totals/ppermute | solution.py:479
  93.7 2.7 %collective-permute-start.4 = (bf16[128,32,128]{2,1,0:T(8,128)(2,1)S(1)}, bf16[128,32,128]{2,1,0:T(8,128)(2,1)S(1)}, u32[]{:S(2)}, u32[]{:S(2)}) collective-permute-start(bf16[128,32,128]{2,1,0:T(8,128)(2,1)S(1)} %get-tuple-element.20), channel_id=1, source_target_pairs={{0,1},{1,0},{2,3},{3,2},{4,5},{5,4},{6,7},{7,6},{8,9},{9,8},{10,11... | collective-permute-start | bytes 3145736 | tf_op jit(solution)/shard_map/exchange_out/ppermute | solution.py:486
